TPU v7x, 32 devices: a whole 2x2x4 slice. The times are simulated.
32 devices in a mesh: beam: 4 (over z), tile: 8 (over y, x, core).
Axes of the slice: x: 2, y: 2, z: 4, core: 2. Of those that a mesh axis runs over, the one named last changes fastest.
Arguments:
- scattering: float32 [16, 2, 1024, 256], P('beam', None, 'tile'), may hold values from -4 to 4
- potential: float32 [1024, 256], P('tile'), may hold values from -6 to 6
- row_offset: int32 [4, 8], P(None, 'tile'), may hold values from 0 to 64
- col_offset: int32 [4, 8], P(None, 'tile'), may hold values from 0 to 128
- table_index: int32 [4, 8], P(None, 'tile'), may hold values from 0 to 3
- beam_tilt: int32 [2, 16], P(None, 'beam'), may hold values from -8 to 8
- coef_table: float32 [2, 4, 16], P(None, None, 'beam'), may hold values from -1.5 to 1.5
- measured: float32 [4, 8, 128, 128], P(None, 'tile'), may hold values from 0 to 2
Outputs:
- residual: float32 [4, 8, 128, 128], P('beam', 'tile')
- gradient: float32 [1024, 256], P('tile')
All inputs are finite; a program needn't handle non-finite values.
Results may differ from a plain program's by a relative error of at most 0.0002.
Values sent between devices are 32-bit elements; how exact they have to be, the bound alone decides.
A program may use at most 64 MiB of HBM per device.

v0:
```python
import math

import jax
import jax.numpy as jnp
from jax import lax
from jax.sharding import PartitionSpec as P

MARGIN = 32


SIGMA_SCALE = 1.0
HIGH = lax.Precision.HIGHEST


def with_halo(cells, sides, width):
    for axis, dim in sides:
        count = lax.axis_size(axis)
        ends = count - 1
        head = lax.slice_in_dim(cells, 0, width, axis=dim)
        tail = lax.slice_in_dim(cells, cells.shape[dim] - width, cells.shape[dim], axis=dim)
        cells = jnp.concatenate(
            [
                lax.ppermute(tail, axis, [(i, (i + 1) % count) for i in range(ends)]),
                cells,
                lax.ppermute(head, axis, [((i + 1) % count, i) for i in range(ends)]),
            ],
            axis=dim,
        )
    return cells


def dft_table(length, inverse):
    pixel_index = jnp.arange(length, dtype=jnp.int32)
    phase_turns = (pixel_index[:, None] * pixel_index[None, :] % length).astype(jnp.float32)
    dft_angle = phase_turns * (2.0 * math.pi / length)
    unit_scale = 1.0 / math.sqrt(length)
    sin_sign = 1.0 if inverse else -1.0
    part_re = jnp.cos(dft_angle) * unit_scale
    part_im = sin_sign * jnp.sin(dft_angle) * unit_scale
    upper = jnp.concatenate([part_re, part_im], 1)
    lower = jnp.concatenate([-part_im, part_re], 1)
    return jnp.concatenate([upper, lower], 0)


def along_last(value_re, value_im, table):
    length = value_re.shape[-1]
    joined = jnp.concatenate([value_re, value_im], -1)
    lead_shape = joined.shape[:-1]
    product = jnp.dot(joined.reshape(-1, 2 * length), table, precision=HIGH)
    product = product.reshape(lead_shape + (2 * length,))
    return (product[..., :length], product[..., length:])


def transform(value_re, value_im, table):
    half_re, half_im = along_last(value_re, value_im, table)
    flip_re = jnp.swapaxes(half_re, -1, -2)
    flip_im = jnp.swapaxes(half_im, -1, -2)
    full_re, full_im = along_last(flip_re, flip_im, table)
    return (jnp.swapaxes(full_re, -1, -2), jnp.swapaxes(full_im, -1, -2))


def finish(summed, start_row, start_col, phase_map, observed, tile_rows, tile_cols):
    patch_len = summed.shape[-1]

    def cut_phase(row_at, col_at):
        return lax.dynamic_slice(phase_map, (row_at, col_at), (patch_len, patch_len))

    local_pot = jax.vmap(cut_phase)(start_row, start_col)
    trans_re = jnp.cos(local_pot)
    trans_im = jnp.sin(local_pot)
    wave_re = summed[:, 0]
    wave_im = summed[:, 1]
    exit_re = trans_re * wave_re - trans_im * wave_im
    exit_im = trans_re * wave_im + trans_im * wave_re
    far_re, far_im = transform(exit_re, exit_im, dft_table(patch_len, False))
    misfit = far_re * far_re + far_im * far_im - observed
    back_re, back_im = transform(misfit * far_re, misfit * far_im, dft_table(patch_len, True))
    pieces = SIGMA_SCALE * (exit_re * back_im - exit_im * back_re)
    offsets = jnp.arange(patch_len, dtype=jnp.int32)
    row_index = start_row[:, None, None] + offsets[None, :, None]
    col_index = start_col[:, None, None] + offsets[None, None, :]
    accum_grid = (
        jnp.zeros((tile_rows + 2 * MARGIN, tile_cols), jnp.float32)
        .at[row_index, col_index]
        .add(pieces)
    )
    return (misfit, accum_grid)


def shards(
    scattering, potential, row_offset, col_offset, table_index, beam_tilt, coef_table, measured
):
    beam_dev = scattering.shape[0]
    tile_rows = scattering.shape[2]
    tile_cols = scattering.shape[3]
    patch_len = measured.shape[-1]
    tile_id = lax.axis_index("tile")
    beam_id = lax.axis_index("beam")
    beam_count = lax.axis_size("beam")
    stacked = jnp.concatenate(
        [scattering.reshape(beam_dev * 2, tile_rows, tile_cols), potential[None]], 0
    )
    extended = with_halo(stacked, (("tile", 1),), MARGIN)
    beam_waves = extended[: 2 * beam_dev].reshape(beam_dev, 2, tile_rows + 2 * MARGIN, tile_cols)
    phase_map = extended[2 * beam_dev] * SIGMA_SCALE
    start_row = row_offset[:, 0]
    start_col = col_offset[:, 0]
    corner_row = start_row + tile_id * tile_rows - MARGIN
    phase_turns = (
        beam_tilt[0][None, :] * corner_row[:, None] + beam_tilt[1][None, :] * start_col[:, None]
    ) % patch_len
    tilt_angle = phase_turns.astype(jnp.float32) * (2.0 * math.pi / patch_len)
    onehot = (
        table_index[:, 0][:, None] == jnp.arange(coef_table.shape[1], dtype=jnp.int32)[None, :]
    ).astype(jnp.float32)
    picked_re = jnp.dot(onehot, coef_table[0], precision=HIGH)
    picked_im = jnp.dot(onehot, coef_table[1], precision=HIGH)
    coef_re = picked_re * jnp.cos(tilt_angle) + picked_im * jnp.sin(tilt_angle)
    coef_im = picked_im * jnp.cos(tilt_angle) - picked_re * jnp.sin(tilt_angle)
    zero_index = jnp.zeros((), jnp.int32)

    def partial_wave(row_at, col_at, weight_re, weight_im):
        region = lax.dynamic_slice(
            beam_waves,
            (zero_index, zero_index, row_at, col_at),
            (beam_dev, 2, patch_len, patch_len),
        )
        wave_re = jnp.einsum("b,bij->ij", weight_re, region[:, 0], precision=HIGH) - jnp.einsum(
            "b,bij->ij", weight_im, region[:, 1], precision=HIGH
        )
        wave_im = jnp.einsum("b,bij->ij", weight_re, region[:, 1], precision=HIGH) + jnp.einsum(
            "b,bij->ij", weight_im, region[:, 0], precision=HIGH
        )
        return jnp.stack([wave_re, wave_im])

    partial_value = jax.vmap(partial_wave)(start_row, start_col, coef_re, coef_im)
    positions = partial_value.shape[0]
    per_beam = positions // beam_count
    first_pos = beam_id * per_beam
    observed_all = measured[:, 0]
    summed = lax.psum_scatter(partial_value, "beam", scatter_dimension=0, tiled=True)
    own_row = lax.dynamic_slice_in_dim(start_row, first_pos, per_beam, 0)
    own_col = lax.dynamic_slice_in_dim(start_col, first_pos, per_beam, 0)
    own_seen = lax.dynamic_slice_in_dim(observed_all, first_pos, per_beam, 0)
    misfit, grad_strip = finish(summed, own_row, own_col, phase_map, own_seen, tile_rows, tile_cols)
    grad_strip = lax.psum(grad_strip, "beam")
    rims = jnp.concatenate([grad_strip[:MARGIN], grad_strip[tile_rows + MARGIN :]], 0)
    beside_all = with_halo(rims, (("tile", 0),), MARGIN)
    core = grad_strip[MARGIN : MARGIN + tile_rows]
    core = core.at[:MARGIN].add(beside_all[:MARGIN])
    core = core.at[tile_rows - MARGIN :].add(beside_all[3 * MARGIN :])
    return (misfit[:, None], core)


def solution(mesh):
    in_specs = (
        P("beam", None, "tile", None),
        P("tile", None),
        P(None, "tile"),
        P(None, "tile"),
        P(None, "tile"),
        P(None, "beam"),
        P(None, None, "beam"),
        P(None, "tile", None, None),
    )
    out_specs = (P("beam", "tile", None, None), P("tile", None))
    return jax.shard_map(shards, mesh=mesh, in_specs=in_specs, out_specs=out_specs, check_vma=False)
```

profile of v0, /device:TPU:1, one launch (start us, length us, event | category | flops | bytes accessed | tf_op | source)
XLA Modules:
  0.0 256.2 jit_solution(14935731644644928338)
XLA Ops:
  8.3 1.6 copy.41
  9.9 1.4 slice_maximum_fusion
  11.3 1.7 copy.44
  13.0 2.0 collective-permute-start.1
  15.3 4.5 %collective-permute-start = (f32[9,32,256]{2,1,0:T(8,128)S(1)}, f32[9,32,256]{2,1,0:T(8,128)}, u32[]{:S(2)}, u32[]{:S(2)}) collective-permute-start(f32[9,32,256]{2,1,0:T(8,128)S(1)} %copy.43), channel_id=1, source_target_pairs={{0,1},{1,2},{2,3},{3,4},{4,5},{5,6},{6,7},{8,9},{9,10},{10,11},{11... | collective-permute-start | bytes 884744 | tf_op jit(solution)/shard_map/ppermute | solution.py:23
  24.0 2.4 copy.45
  26.4 3.4 %pad_maximum_fusion = f32[8,192,256]{1,2,0:T(8,128)} fusion(f32[9,32,256]{1,2,0:T(8,128)S(1)} %copy.46, f32[9,32,256]{1,2,0:T(8,128)} %copy.45, f32[1,128,256]{1,2,0:T(8,128)S(1)} %bitcast.145, f32[8,128,256]{1,2,0:T(8,128)S(1)} %bitcast.141), kind=kLoop, calls=%fused_computation.4 | loop fusion | flops 1179648 | bytes 3342336 | tf_op jit(solution)/shard_map/concatenate | solution.py:21
  29.9 17.1 %while.4 = (s32[]{:T(128)}, f32[4,2,192,256]{2,3,1,0:T(8,128)}, s32[4,4]{1,0:T(4,128)S(1)}, f32[4,4,2,128,128]{4,3,2,1,0:T(8,128)}, s32[]{:T(128)}) while((s32[]{:T(128)}, f32[4,2,192,256]{2,3,1,0:T(8,128)}, s32[4,4]{1,0:T(4,128)S(1)}, f32[4,4,2,128,128]{4,3,2,1,0:T(8,128)}, s32[]{:T(128)}) %tuple.64), condition=%wide.while_cond.3, body=%wide.while_body.3.sunk | while | flops 2 | bytes 3145861 | solution.py:123
  30.5 2.6 %constant_dynamic-slice_fusion.8 = f32[4,2,128,128]{2,3,1,0:T(8,128)S(1)} fusion(f32[4,2,192,256]{2,3,1,0:T(8,128)} %get-tuple-element.143, s32[]{:T(128)} %bitcast.138, s32[]{:T(128)} %bitcast.139), kind=kLoop, calls=%fused_computation.2.clone.1 | loop fusion | bytes 1048584 | tf_op jit(solution)/shard_map/vmap()/gather
  34.8 2.6 %constant_dynamic-slice_fusion.8 = f32[4,2,128,128]{2,3,1,0:T(8,128)S(1)} fusion(f32[4,2,192,256]{2,3,1,0:T(8,128)} %get-tuple-element.143, s32[]{:T(128)} %bitcast.138, s32[]{:T(128)} %bitcast.139), kind=kLoop, calls=%fused_computation.2.clone.1 | loop fusion | bytes 1048584 | tf_op jit(solution)/shard_map/vmap()/gather
  39.0 2.6 %constant_dynamic-slice_fusion.8 = f32[4,2,128,128]{2,3,1,0:T(8,128)S(1)} fusion(f32[4,2,192,256]{2,3,1,0:T(8,128)} %get-tuple-element.143, s32[]{:T(128)} %bitcast.138, s32[]{:T(128)} %bitcast.139), kind=kLoop, calls=%fused_computation.2.clone.1 | loop fusion | bytes 1048584 | tf_op jit(solution)/shard_map/vmap()/gather
  43.3 2.6 %constant_dynamic-slice_fusion.8 = f32[4,2,128,128]{2,3,1,0:T(8,128)S(1)} fusion(f32[4,2,192,256]{2,3,1,0:T(8,128)} %get-tuple-element.143, s32[]{:T(128)} %bitcast.138, s32[]{:T(128)} %bitcast.139), kind=kLoop, calls=%fused_computation.2.clone.1 | loop fusion | bytes 1048584 | tf_op jit(solution)/shard_map/vmap()/gather
  46.9 1.7 slice_bitcast_fusion
  48.6 2.4 fusion.4
  51.0 2.4 fusion.2
  53.4 3.1 %fusion = f32[4,1,128,128]{3,1,2,0:T(1,128)} fusion(f32[4,4,1,1]{1,2,3,0:T(1,128)S(1)} %bitcast.149, f32[4,4,128,128]{3,2,1,0:T(8,128)S(1)} %get-tuple-element.77), kind=kOutput, calls=%fused_computation.15 | convolution fusion | flops 3145728 | bytes 1310784 | tf_op jit(solution)/shard_map/vmap(b,bij->ij)/dot_general | solution.py:131
  56.5 2.4 fusion.6
  64.0 1.3 compare_select_fusion
  71.3 14.8 %reduce-scatter.2.cloned.1.call-done = f32[1,2,128,128]{2,3,1,0:T(8,128)} async-done(((f32[4,2,128,128]{2,3,1,0:T(8,128)}), f32[1,2,128,128]{2,3,1,0:T(8,128)}) %reduce-scatter.2.cloned.1.call-update) | async-done | bytes 131088 | tf_op jit(solution)/shard_map/reduce_scatter | solution.py:141
  89.0 113.6 %scatter_custom_fusion = f32[49152]{0:T(1024)S(1)} fusion(s32[16384]{0:T(1024)S(1)} %select_bitcast_fusion, f32[16384]{0:T(1024)S(1)} %bitcast.148, f32[]{:T(128)} %constant.121.clone.1), kind=kCustom, calls=%fused_computation.57 | custom fusion | flops 16384 | bytes 196612
  203.3 33.1 %all-reduce.2.cloned.1.call-done = f32[192,256]{1,0:T(8,128)} async-done(((f32[192,256]{1,0:T(8,128)}), f32[192,256]{1,0:T(8,128)}) %all-reduce.2.cloned.1.call-update) | async-done | bytes 196624 | tf_op jit(solution)/shard_map/psum | solution.py:146
  237.3 5.5 %collective-permute-start.2 = (f32[32,256]{1,0:T(8,128)S(1)}, f32[32,256]{1,0:T(8,128)S(1)}, u32[]{:S(2)}, u32[]{:S(2)}) collective-permute-start(f32[32,256]{1,0:T(8,128)S(1)} %get-tuple-element.84), channel_id=1, source_target_pairs={{0,1},{1,2},{2,3},{3,4},{4,5},{5,6},{6,7},{8,9},{9,10},{10,11},{11... | collective-permute-start | bytes 98312 | tf_op jit(solution)/shard_map/ppermute | solution.py:23
  243.4 1.9 collective-permute-start.3
  247.1 1.6 collective-permute-done.3
  (107 shorter events, 26.9 us)
Async XLA Ops:
  7.2 15.7 %copy-start = (f32[4,1,128,128]{3,2,1,0:T(8,128)S(1)}, f32[4,1,128,128]{3,2,1,0:T(8,128)}, u32[]{:S(2)}) copy-start(f32[4,1,128,128]{3,2,1,0:T(8,128)} %param.19) | copy-start | bytes 786436
  7.2 78.9 %reduce-scatter.2.cloned.1.call-start = ((), (), s32[]{:S(2)}) async-start(), calls=%async_computation.1 | async-start | bytes 655360 | tf_op jit(solution)/shard_map/reduce_scatter | solution.py:141
  8.3 18.2 %copy-start.1 = (f32[128,256]{0,1:T(8,128)}, f32[128,256]{0,1:T(8,128)S(1)}, u32[]{:S(2)}) copy-start(f32[128,256]{0,1:T(8,128)S(1)} %copy.42) | copy-start | bytes 393220
  11.3 9.4 %copy-start.6 = (s32[4,1]{0,1:T(1,128)S(1)}, s32[4,1]{0,1:T(1,128)}, u32[]{:S(2)}) copy-start(s32[4,1]{0,1:T(1,128)} %param.14) | copy-start | bytes 52
  11.3 9.9 %copy-start.7 = (s32[4,1]{0,1:T(1,128)S(1)}, s32[4,1]{0,1:T(1,128)}, u32[]{:S(2)}) copy-start(s32[4,1]{0,1:T(1,128)} %param.15) | copy-start | bytes 52
  11.3 10.8 %copy-start.8 = (s32[2,4]{1,0:T(2,128)S(1)}, s32[2,4]{1,0:T(2,128)}, u32[]{:S(2)}) copy-start(s32[2,4]{1,0:T(2,128)} %param.17) | copy-start | bytes 100
  11.3 11.2 %copy-start.11 = (f32[2,4,4]{2,1,0:T(4,128)S(1)}, f32[2,4,4]{2,1,0:T(4,128)}, u32[]{:S(2)}) copy-start(f32[2,4,4]{2,1,0:T(4,128)} %param.18) | copy-start | bytes 388
  11.3 11.2 %copy-start.12 = (s32[4,1]{0,1:T(1,128)S(1)}, s32[4,1]{0,1:T(1,128)}, u32[]{:S(2)}) copy-start(s32[4,1]{0,1:T(1,128)} %param.16) | copy-start | bytes 52
  13.0 10.6 %collective-permute-start.1 = (f32[9,32,256]{2,1,0:T(8,128)S(1)}, f32[9,32,256]{2,1,0:T(8,128)S(1)}, u32[]{:S(2)}, u32[]{:S(2)}) collective-permute-start(f32[9,32,256]{2,1,0:T(8,128)S(1)} %copy.44), channel_id=1, source_target_pairs={{1,0},{2,1},{3,2},{4,3},{5,4},{6,5},{7,6},{9,8},{10,9},{11,10},{12... | collective-permute-start | bytes 884744 | tf_op jit(solution)/shard_map/ppermute | solution.py:25
  15.3 8.7 %collective-permute-start = (f32[9,32,256]{2,1,0:T(8,128)S(1)}, f32[9,32,256]{2,1,0:T(8,128)}, u32[]{:S(2)}, u32[]{:S(2)}) collective-permute-start(f32[9,32,256]{2,1,0:T(8,128)S(1)} %copy.43), channel_id=1, source_target_pairs={{0,1},{1,2},{2,3},{3,4},{4,5},{5,6},{6,7},{8,9},{9,10},{10,11},{11... | collective-permute-start | bytes 884744 | tf_op jit(solution)/shard_map/ppermute | solution.py:23
  60.9 8.9 %copy-start.10 = (s32[2]{0:T(128)S(1)}, s32[2]{0:T(128)}, u32[]{:S(2)}) copy-start(s32[2]{0:T(128)} %constant.127) | copy-start | bytes 28
  60.9 9.0 %copy-start.9 = (s32[2]{0:T(128)S(1)}, s32[2]{0:T(128)}, u32[]{:S(2)}) copy-start(s32[2]{0:T(128)} %constant.130) | copy-start | bytes 28
  61.8 8.3 %copy-start.2 = (f32[128,256]{0,1:T(8,128)S(1)}, f32[128,256]{0,1:T(8,128)}, u32[]{:S(2)}) copy-start(f32[128,256]{0,1:T(8,128)} %copy-done.1) | copy-start | bytes 393220
  61.8 6.0 %copy-start.3 = (f32[1,1,128,128]{3,2,1,0:T(8,128)S(1)}, f32[1,1,128,128]{3,2,1,0:T(8,128)}, u32[]{:S(2)}) copy-start(f32[1,1,128,128]{3,2,1,0:T(8,128)} %constant_dynamic-slice_fusion.2) | copy-start | bytes 196612
  63.8 172.7 %all-reduce.2.cloned.1.call-start = ((), (), s32[]{:S(2)}) async-start(), calls=%async_computation.2 | async-start | bytes 393216 | tf_op jit(solution)/shard_map/psum | solution.py:146
  70.0 17.2 %copy-start.5 = (f32[128,128]{1,0:T(8,128)S(1)}, f32[128,128]{1,0:T(8,128)}, u32[]{:S(2)}) copy-start(f32[128,128]{1,0:T(8,128)} %fusion.50) | copy-start | bytes 196612
  237.3 9.0 %collective-permute-start.2 = (f32[32,256]{1,0:T(8,128)S(1)}, f32[32,256]{1,0:T(8,128)S(1)}, u32[]{:S(2)}, u32[]{:S(2)}) collective-permute-start(f32[32,256]{1,0:T(8,128)S(1)} %get-tuple-element.84), channel_id=1, source_target_pairs={{0,1},{1,2},{2,3},{3,4},{4,5},{5,6},{6,7},{8,9},{9,10},{10,11},{11... | collective-permute-start | bytes 98312 | tf_op jit(solution)/shard_map/ppermute | solution.py:23
  243.4 5.2 %collective-permute-start.3 = (f32[32,256]{1,0:T(8,128)S(1)}, f32[32,256]{1,0:T(8,128)S(1)}, u32[]{:S(2)}, u32[]{:S(2)}) collective-permute-start(f32[32,256]{1,0:T(8,128)S(1)} %get-tuple-element.83), channel_id=1, source_target_pairs={{1,0},{2,1},{3,2},{4,3},{5,4},{6,5},{7,6},{9,8},{10,9},{11,10},{12... | collective-permute-start | bytes 98312 | tf_op jit(solution)/shard_map/ppermute | solution.py:25
  248.7 0.7 copy-start.4
Sparse Core Ops, SparseCore 0:
  63.9 22.1 reduce-scatter.1
  203.4 32.9 all-reduce.1
where the time goes:
time: 257 us; the launch traced here: 256 us
  other arithmetic  127 us (49%)
  waiting for transfers between devices  49.6 us (19%)
  local copies, waits for them, and re-layouts  35.6 us (14%)
  between operations  18.2 us (7%)
  starting transfers between devices  14.1 us (5%)
  matrix products  12.1 us (5%)
    unnamed x5, other arithmetic  114 us
    psum x1, waiting for transfers between devices, shards(): grad_strip = lax.psum(grad_strip, 'beam')  33.1 us
    gather x20, local copies, waits for them, and re-layouts  17 us
    reduce_scatter x1, waiting for transfers between devices, shards(): lax.psum_scatter(partial_value, 'beam', scatter_dimension=0, tiled=True)  14.8 us
    ppermute x2, starting transfers between devices, with_halo(): lax.ppermute(tail, axis, [(i, (i + 1) % count) for i in range(ends)])  9.91 us
  transfers between devices with their start and end apart: 6, of which 3 were waited for; matrix products, arithmetic and copies ran while one was open for 4% of the time, Pallas kernels for 0%

commit v1 on v0

v1 whole, which is shorter than its diff:
```python
import functools
import math

import jax
import jax.numpy as jnp
import numpy as np
from jax import lax
from jax.experimental import pallas as pl
from jax.experimental.pallas import tpu as pltpu
from jax.sharding import PartitionSpec as P

MARGIN = 32
SIGMA_SCALE = 1.0
MESH = pl.DeviceIdType.MESH


def tables(length):
    index = np.arange(length)
    angle = (index[:, None] * index[None, :] % length) * (2.0 * math.pi / length)
    re = np.cos(angle) / math.sqrt(length)
    im = -np.sin(angle) / math.sqrt(length)
    ahead = np.block([[re, im], [-im, re]]).astype(np.float32)
    back = np.block([[re, -im], [im, re]]).astype(np.float32)
    both = np.stack([ahead, back])
    high = both.astype(jnp.bfloat16)
    low = (both - high.astype(np.float32)).astype(jnp.bfloat16)
    turns = np.arange(length) * (2.0 * math.pi / length)
    trig = np.stack([np.cos(turns), np.sin(turns)]).astype(np.float32)
    return high, low, trig


def split(value):
    high = value.astype(jnp.bfloat16)
    low = (value - high.astype(jnp.float32)).astype(jnp.bfloat16)
    return high, low


def dot(left, right):
    return jnp.dot(left, right, preferred_element_type=jnp.float32)


def split_dot(left, right):
    return dot(left[0], right[0]) + (dot(left[0], right[1]) + dot(left[1], right[0]))


def transform(stacked, left_table, right_table):
    length = stacked.shape[-1]
    half = split_dot(left_table, split(stacked))
    wide = jnp.concatenate([half[:length], half[length:]], 1)
    return split_dot(split(wide), right_table)


def kernel(
    n,
    tiles,
    row_ref,
    col_ref,
    index_ref,
    tilt_ref,
    coef_ref,
    trig_ref,
    high_ref,
    low_ref,
    scat,
    pot,
    meas,
    misfit_ref,
    grad_ref,
    loc,
    ploc,
    halo,
    phalo,
    seen,
    block,
    send_b,
    recv_a,
    recv_b,
    trans,
    piece,
    recv_p,
    strip,
    rims,
    local_sem,
    halo_send,
    halo_recv,
    a_send,
    a_recv,
    b_send,
    b_recv,
    p_send,
    p_recv,
    rim_send,
    rim_recv,
):
    me = lax.axis_index("beam")
    tile = lax.axis_index("tile")
    beams = scat.shape[0]
    rows, cols = scat.shape[2], scat.shape[3]
    patch = seen.shape[-1]
    middle = patch - 2 * MARGIN

    local = [
        pltpu.make_async_copy(scat, loc, local_sem.at[0]),
        pltpu.make_async_copy(pot, ploc, local_sem.at[1]),
        pltpu.make_async_copy(meas.at[me, 0], seen, local_sem.at[2]),
    ]
    for copy in local:
        copy.start()

    barrier = pltpu.get_barrier_semaphore()
    for k in range(1, n):
        pl.semaphore_signal(
            barrier, inc=1, device_id={"beam": lax.rem(me + k, n)}, device_id_type=MESH
        )
    has_up = tile > 0
    has_down = tile < tiles - 1

    @pl.when(has_up)
    def _():
        pl.semaphore_signal(barrier, inc=1, device_id={"tile": tile - 1}, device_id_type=MESH)

    @pl.when(has_down)
    def _():
        pl.semaphore_signal(barrier, inc=1, device_id={"tile": tile + 1}, device_id_type=MESH)

    pl.semaphore_wait(barrier, n - 1 + has_up.astype(jnp.int32) + has_down.astype(jnp.int32))

    def remote(src, dst, send_sem, recv_sem, where):
        return pltpu.make_async_remote_copy(
            src_ref=src,
            dst_ref=dst,
            send_sem=send_sem,
            recv_sem=recv_sem,
            device_id=where,
            device_id_type=MESH,
        )

    last = pl.ds(rows - MARGIN, MARGIN)
    first = pl.ds(0, MARGIN)
    second = pl.ds(MARGIN, MARGIN)
    below = pl.ds(rows + MARGIN, MARGIN)
    up = [
        remote(scat.at[:, :, first, :], halo.at[:, :, second, :], halo_send.at[0], halo_recv.at[0], {"tile": tile - 1}),
        remote(pot.at[first, :], phalo.at[second, :], halo_send.at[1], halo_recv.at[1], {"tile": tile - 1}),
    ]
    down = [
        remote(scat.at[:, :, last, :], halo.at[:, :, first, :], halo_send.at[2], halo_recv.at[2], {"tile": tile + 1}),
        remote(pot.at[last, :], phalo.at[first, :], halo_send.at[3], halo_recv.at[3], {"tile": tile + 1}),
    ]

    @pl.when(has_up)
    def _():
        for copy in up:
            copy.start()

    @pl.when(has_down)
    def _():
        for copy in down:
            copy.start()

    @pl.when(tile == 0)
    def _():
        halo[:, :, :MARGIN, :] = jnp.zeros((beams, 2, MARGIN, cols), jnp.float32)
        phalo[:MARGIN, :] = jnp.zeros((MARGIN, cols), jnp.float32)

    @pl.when(tile == tiles - 1)
    def _():
        halo[:, :, MARGIN:, :] = jnp.zeros((beams, 2, MARGIN, cols), jnp.float32)
        phalo[MARGIN:, :] = jnp.zeros((MARGIN, cols), jnp.float32)

    def weights(p):
        corner = row_ref[p] + tile * rows - MARGIN
        picked = index_ref[p]
        result = []
        for b in range(beams):
            turn = (tilt_ref[0, b] * corner + tilt_ref[1, b] * col_ref[p]) & (patch - 1)
            cos, sin = trig_ref[0, turn], trig_ref[1, turn]
            q_re = coef_ref[picked, b]
            q_im = coef_ref[picked + coef_ref.shape[0] // 2, b]
            result.append((q_re * cos + q_im * sin, q_im * cos - q_re * sin))
        return result

    def iota(shape, axis):
        return lax.broadcasted_iota(jnp.int32, shape, axis)

    def ones(mask):
        return jnp.where(mask, 1.0, 0.0).astype(jnp.bfloat16)

    def pick_cols(p):
        shape = (cols, patch)
        return ones(iota(shape, 0) - iota(shape, 1) == col_ref[p])

    def pick_rows(p):
        shape = (patch, rows)
        return ones(iota(shape, 1) - iota(shape, 0) == row_ref[p] - MARGIN)

    def pick_halo(p, out_rows):
        shape = (out_rows, 2 * MARGIN)
        held = iota(shape, 1)
        held = jnp.where(held < MARGIN, held, held + rows)
        wanted = iota(shape, 0)
        if out_rows < patch:
            wanted = jnp.where(wanted < MARGIN, wanted, wanted + middle)
        return ones(held - wanted == row_ref[p])

    def combine(source, count, coefs):
        total_re = total_im = None
        for b in range(beams):
            re = source[b, 0, :count, :]
            im = source[b, 1, :count, :]
            c_re, c_im = coefs[b]
            now_re = c_re * re - c_im * im
            now_im = c_re * im + c_im * re
            total_re = now_re if total_re is None else total_re + now_re
            total_im = now_im if total_im is None else total_im + now_im
        return jnp.concatenate(split(total_re) + split(total_im), 0)

    def block_of(combined, col_pick, row_pick):
        count = combined.shape[0] // 4
        chosen = dot(combined, col_pick).astype(jnp.bfloat16)
        chosen = jnp.concatenate([chosen[: 2 * count], chosen[2 * count :]], 1)
        return dot(jnp.concatenate([row_pick, row_pick], 1), chosen)

    order = list(range(1, n))
    coefs = {}
    col_picks = {}
    copies_a, copies_b = {}, {}
    local[0].wait()
    for k in order + [0]:
        p = lax.rem(me + k, n)
        coefs[k] = weights(p)
        col_picks[k] = pick_cols(p)
        got = block_of(combine(loc, rows, coefs[k]), col_picks[k], pick_rows(p))
        block[k, 0] = got[:, :patch]
        block[k, 1] = got[:, patch:]
        if k != 0:
            copies_a[k] = remote(
                block.at[k, :, pl.ds(MARGIN, middle), :],
                recv_a.at[k - 1],
                a_send.at[k - 1],
                a_recv.at[k - 1],
                {"beam": p},
            )
            copies_a[k].start()

    local[1].wait()

    @pl.when(has_down)
    def _():
        for copy in up:
            copy.wait_recv()

    @pl.when(has_up)
    def _():
        for copy in down:
            copy.wait_recv()

    for k in order + [0]:
        p = lax.rem(me + k, n)
        got = block_of(combine(halo, 2 * MARGIN, coefs[k]), col_picks[k], pick_halo(p, 2 * MARGIN))
        for c in range(2):
            part = got[:, c * patch : (c + 1) * patch]
            send_b[k, c, :MARGIN, :] = block[k, c, :MARGIN, :] + part[:MARGIN]
            send_b[k, c, MARGIN:, :] = block[k, c, MARGIN + middle :, :] + part[MARGIN:]
        if k != 0:
            copies_b[k] = remote(
                send_b.at[k], recv_b.at[k - 1], b_send.at[k - 1], b_recv.at[k - 1], {"beam": p}
            )
            copies_b[k].start()

    tall = jnp.concatenate([ploc[...], phalo[...]], 0)
    high, low = split(tall)
    least = (tall - high.astype(jnp.float32) - low.astype(jnp.float32)).astype(jnp.bfloat16)
    row_pick = jnp.concatenate([pick_rows(me), pick_halo(me, patch)], 1)
    here = None
    for term in (least, low, high):
        now = dot(row_pick, dot(term, col_picks[0]).astype(jnp.bfloat16))
        here = now if here is None else here + now
    here = here * SIGMA_SCALE
    trans[0] = jnp.cos(here)
    trans[1] = jnp.sin(here)

    for k in order:
        copies_a[k].wait_recv()
        copies_b[k].wait_recv()
    local[2].wait()

    parts = []
    for c in range(2):
        mid = block[0, c, MARGIN : MARGIN + middle, :]
        head = send_b[0, c, :MARGIN, :]
        tail = send_b[0, c, MARGIN:, :]
        for k in order:
            mid += recv_a[k - 1, c]
            head += recv_b[k - 1, c, :MARGIN, :]
            tail += recv_b[k - 1, c, MARGIN:, :]
        parts.append(jnp.concatenate([head, mid, tail], 0))
    wave_re, wave_im = parts
    exit_re = trans[0] * wave_re - trans[1] * wave_im
    exit_im = trans[0] * wave_im + trans[1] * wave_re
    ahead = (high_ref[0], low_ref[0])
    back = (high_ref[1], low_ref[1])
    far = transform(jnp.concatenate([exit_re, exit_im], 0), back, ahead)
    far_re, far_im = far[:, :patch], far[:, patch:]
    misfit = far_re * far_re + far_im * far_im - seen[...]
    misfit_ref[...] = misfit
    turned = transform(jnp.concatenate([misfit * far_re, misfit * far_im], 0), ahead, back)
    piece[...] = SIGMA_SCALE * (exit_re * turned[:, patch:] - exit_im * turned[:, :patch])

    copies_p = {}
    for k in order:
        copies_p[k] = remote(
            piece, recv_p.at[k - 1], p_send.at[k - 1], p_recv.at[k - 1], {"beam": lax.rem(me + k, n)}
        )
        copies_p[k].start()

    def place(value, p):
        shape = (patch, cols)
        col_place = ones(iota(shape, 1) - iota(shape, 0) == col_ref[p])
        shape = (rows + 2 * MARGIN, patch)
        row_place = ones(iota(shape, 0) - iota(shape, 1) == row_ref[p])
        moved = dot(jnp.concatenate(split(value), 0), col_place).astype(jnp.bfloat16)
        return dot(jnp.concatenate([row_place, row_place], 1), moved)

    strip[...] = place(piece[...], me)
    for k in order:
        copies_p[k].wait_recv()
        strip[...] += place(recv_p[k - 1], lax.rem(me + n - k, n))

    rim_up = remote(strip.at[first, :], rims.at[1], rim_send.at[0], rim_recv.at[0], {"tile": tile - 1})
    rim_down = remote(strip.at[below, :], rims.at[0], rim_send.at[1], rim_recv.at[1], {"tile": tile + 1})

    @pl.when(has_up)
    def _():
        rim_up.start()

    @pl.when(has_down)
    def _():
        rim_down.start()

    grad_ref[...] = strip[MARGIN : MARGIN + rows, :]

    @pl.when(has_down)
    def _():
        rim_up.wait_recv()
        grad_ref[rows - MARGIN :, :] += rims[1]

    @pl.when(has_up)
    def _():
        rim_down.wait_recv()
        grad_ref[:MARGIN, :] += rims[0]

    for k in order:
        copies_a[k].wait_send()
        copies_b[k].wait_send()
        copies_p[k].wait_send()

    @pl.when(has_up)
    def _():
        for copy in up + [rim_up]:
            copy.wait_send()

    @pl.when(has_down)
    def _():
        for copy in down + [rim_down]:
            copy.wait_send()


def shards(
    n,
    tiles,
    scattering,
    potential,
    row_offset,
    col_offset,
    table_index,
    beam_tilt,
    coef_table,
    measured,
):
    beams, _, rows, cols = scattering.shape
    positions, patch = measured.shape[0], measured.shape[-1]
    assert positions == n and patch & (patch - 1) == 0 and cols & (cols - 1) == 0
    high, low, trig = tables(patch)
    f32 = jnp.float32
    middle = patch - 2 * MARGIN
    smem = pl.BlockSpec(memory_space=pltpu.SMEM)
    vmem = pl.BlockSpec(memory_space=pltpu.VMEM)
    anywhere = pl.BlockSpec(memory_space=pl.ANY)
    strip_rows = rows + 2 * MARGIN
    dma = pltpu.SemaphoreType.DMA
    misfit, grad = pl.pallas_call(
        functools.partial(kernel, n, tiles),
        out_shape=(
            jax.ShapeDtypeStruct((patch, patch), f32),
            jax.ShapeDtypeStruct((rows, cols), f32),
        ),
        in_specs=[smem] * 6 + [vmem] * 2 + [anywhere] * 3,
        out_specs=(vmem, vmem),
        scratch_shapes=[
            pltpu.VMEM((beams, 2, rows, cols), f32),
            pltpu.VMEM((rows, cols), f32),
            pltpu.VMEM((beams, 2, 2 * MARGIN, cols), f32),
            pltpu.VMEM((2 * MARGIN, cols), f32),
            pltpu.VMEM((patch, patch), f32),
            pltpu.VMEM((n, 2, patch, patch), f32),
            pltpu.VMEM((n, 2, 2 * MARGIN, patch), f32),
            pltpu.VMEM((n - 1, 2, middle, patch), f32),
            pltpu.VMEM((n - 1, 2, 2 * MARGIN, patch), f32),
            pltpu.VMEM((2, patch, patch), f32),
            pltpu.VMEM((patch, patch), f32),
            pltpu.VMEM((n - 1, patch, patch), f32),
            pltpu.VMEM((strip_rows, cols), f32),
            pltpu.VMEM((2, MARGIN, cols), f32),
            dma((3,)),
            dma((4,)),
            dma((4,)),
            dma((n - 1,)),
            dma((n - 1,)),
            dma((n - 1,)),
            dma((n - 1,)),
            dma((n - 1,)),
            dma((n - 1,)),
            dma((2,)),
            dma((2,)),
        ],
        compiler_params=pltpu.CompilerParams(
            collective_id=0, has_side_effects=True, vmem_limit_bytes=56 * 1024 * 1024
        ),
    )(
        row_offset[:, 0],
        col_offset[:, 0],
        table_index[:, 0],
        beam_tilt,
        coef_table.reshape(-1, beams),
        trig,
        high,
        low,
        scattering,
        potential,
        measured,
    )
    return misfit[None, None], grad


def solution(mesh):
    in_specs = (
        P("beam", None, "tile", None),
        P("tile", None),
        P(None, "tile"),
        P(None, "tile"),
        P(None, "tile"),
        P(None, "beam"),
        P(None, None, "beam"),
        P(None, "tile", None, None),
    )
    out_specs = (P("beam", "tile", None, None), P("tile", None))
    run = functools.partial(shards, mesh.shape["beam"], mesh.shape["tile"])
    return jax.shard_map(run, mesh=mesh, in_specs=in_specs, out_specs=out_specs, check_vma=False)
```

time: 257 us -> 34.1 us (0.13)
  the two profiles are of different devices: /device:TPU:1 before, /device:TPU:3 now
where the time goes in v1:
time: 34.1 us; the launch traced here: 34 us
  Pallas kernels  31.1 us (91%)
  local copies, waits for them, and re-layouts  2.17 us (6%)
  between operations  0.65 us (2%)
    pallas_call x1, Pallas kernels, shards(): pl.pallas_call(functools.partial(kernel, n, tiles), out_shape=(jax.ShapeD...  31.1 us
    unnamed x4, local copies, waits for them, and re-layouts  2.17 us

profile of v1, /device:TPU:3, one launch (start us, length us, event | category | flops | bytes accessed | tf_op | source)
XLA Modules:
  0.0 34.0 jit_solution(13672101569103048959)
XLA Ops:
  0.6 31.1 %shard_map.122 = (f32[128,128]{1,0:T(8,128)}, f32[128,256]{1,0:T(8,128)}) custom-call(s32[4]{0:T(128)} %bitcast.7, s32[4]{0:T(128)} %bitcast.8, s32[4]{0:T(128)} %bitcast.9, s32[2,4]{1,0:T(2,128)} %tilt_ref.1, f32[8,4]{1,0:T(8,128)} %bitcast.6, f32[2,128]{1,0:T(2,128)} %constant.6.clone.trig_ref, bf16[2,256,256]{2,1,0:T(8,128)(2,1)} %constant.7.clone.high_ref, ...), custom_call_target="tpu_custom_call" | custom-call | tf_op jit(solution)/shard_map/pallas_call | solution.py:392
  31.8 0.0 copy-start
  31.8 1.5 %copy.18 = f32[1,1,128,128]{3,2,1,0:T(8,128)} copy(f32[1,1,128,128]{3,2,1,0:T(8,128)} %bitcast.5) | data formatting | bytes 131072
  33.3 0.0 copy-done
  33.3 0.7 %copy.19 = f32[128,256]{1,0:T(8,128)} copy(f32[128,256]{1,0:T(8,128)S(1)} %copy-done) | data formatting | bytes 262144
Async XLA Ops:
  31.8 1.5 %copy-start = (f32[128,256]{1,0:T(8,128)S(1)}, f32[128,256]{1,0:T(8,128)}, u32[]{:S(2)}) copy-start(f32[128,256]{1,0:T(8,128)} %get-tuple-element.9) | copy-start | bytes 393220

commit v2 on v1

--- a/solution.py
+++ b/solution.py
@@ -68,6 +68,10 @@
     grad_ref,
     loc,
     ploc,
+    mine,
+    from_above,
+    from_below,
+    edge,
     halo,
     phalo,
     seen,
@@ -139,41 +143,47 @@
     first = pl.ds(0, MARGIN)
     second = pl.ds(MARGIN, MARGIN)
     below = pl.ds(rows + MARGIN, MARGIN)
+    for p in range(n):
+        mine[0, p] = row_ref[p]
+        mine[1, p] = col_ref[p]
+        mine[2, p] = index_ref[p]
+    to_up, to_down = {"tile": tile - 1}, {"tile": tile + 1}
     up = [
-        remote(scat.at[:, :, first, :], halo.at[:, :, second, :], halo_send.at[0], halo_recv.at[0], {"tile": tile - 1}),
-        remote(pot.at[first, :], phalo.at[second, :], halo_send.at[1], halo_recv.at[1], {"tile": tile - 1}),
+        remote(mine, from_below, halo_send.at[0], halo_recv.at[0], to_up),
+        remote(pot.at[first, :], phalo.at[second, :], halo_send.at[1], halo_recv.at[1], to_up),
+        remote(edge.at[1], halo.at[1], halo_send.at[2], halo_recv.at[2], to_up),
     ]
     down = [
-        remote(scat.at[:, :, last, :], halo.at[:, :, first, :], halo_send.at[2], halo_recv.at[2], {"tile": tile + 1}),
-        remote(pot.at[last, :], phalo.at[first, :], halo_send.at[3], halo_recv.at[3], {"tile": tile + 1}),
+        remote(mine, from_above, halo_send.at[3], halo_recv.at[3], to_down),
+        remote(pot.at[last, :], phalo.at[first, :], halo_send.at[4], halo_recv.at[4], to_down),
+        remote(edge.at[0], halo.at[0], halo_send.at[5], halo_recv.at[5], to_down),
     ]
 
     @pl.when(has_up)
     def _():
-        for copy in up:
-            copy.start()
-
-    @pl.when(has_down)
-    def _():
-        for copy in down:
-            copy.start()
+        up[0].start()
+        up[1].start()
+
+    @pl.when(has_down)
+    def _():
+        down[0].start()
+        down[1].start()
 
     @pl.when(tile == 0)
     def _():
-        halo[:, :, :MARGIN, :] = jnp.zeros((beams, 2, MARGIN, cols), jnp.float32)
+        halo[0] = jnp.zeros(halo.shape[1:], jnp.float32)
         phalo[:MARGIN, :] = jnp.zeros((MARGIN, cols), jnp.float32)
 
     @pl.when(tile == tiles - 1)
     def _():
-        halo[:, :, MARGIN:, :] = jnp.zeros((beams, 2, MARGIN, cols), jnp.float32)
+        halo[1] = jnp.zeros(halo.shape[1:], jnp.float32)
         phalo[MARGIN:, :] = jnp.zeros((MARGIN, cols), jnp.float32)
 
-    def weights(p):
-        corner = row_ref[p] + tile * rows - MARGIN
-        picked = index_ref[p]
+    def weights(row_at, col_at, picked, tile_at):
+        corner = row_at + tile_at * rows - MARGIN
         result = []
         for b in range(beams):
-            turn = (tilt_ref[0, b] * corner + tilt_ref[1, b] * col_ref[p]) & (patch - 1)
+            turn = (tilt_ref[0, b] * corner + tilt_ref[1, b] * col_at) & (patch - 1)
             cos, sin = trig_ref[0, turn], trig_ref[1, turn]
             q_re = coef_ref[picked, b]
             q_im = coef_ref[picked + coef_ref.shape[0] // 2, b]
@@ -186,28 +196,25 @@
     def ones(mask):
         return jnp.where(mask, 1.0, 0.0).astype(jnp.bfloat16)
 
-    def pick_cols(p):
+    def pick_cols(col_at):
         shape = (cols, patch)
-        return ones(iota(shape, 0) - iota(shape, 1) == col_ref[p])
-
-    def pick_rows(p):
+        return ones(iota(shape, 0) - iota(shape, 1) == col_at)
+
+    def pick_rows(row_at):
         shape = (patch, rows)
-        return ones(iota(shape, 1) - iota(shape, 0) == row_ref[p] - MARGIN)
-
-    def pick_halo(p, out_rows):
-        shape = (out_rows, 2 * MARGIN)
+        return ones(iota(shape, 1) - iota(shape, 0) == row_at - MARGIN)
+
+    def pick_halo(row_at):
+        shape = (patch, 2 * MARGIN)
         held = iota(shape, 1)
         held = jnp.where(held < MARGIN, held, held + rows)
-        wanted = iota(shape, 0)
-        if out_rows < patch:
-            wanted = jnp.where(wanted < MARGIN, wanted, wanted + middle)
-        return ones(held - wanted == row_ref[p])
-
-    def combine(source, count, coefs):
+        return ones(held - iota(shape, 0) == row_at)
+
+    def combine(source, at, count, coefs):
         total_re = total_im = None
         for b in range(beams):
-            re = source[b, 0, :count, :]
-            im = source[b, 1, :count, :]
+            re = source[b, 0, at : at + count, :]
+            im = source[b, 1, at : at + count, :]
             c_re, c_im = coefs[b]
             now_re = c_re * re - c_im * im
             now_im = c_re * im + c_im * re
@@ -222,46 +229,67 @@
         return dot(jnp.concatenate([row_pick, row_pick], 1), chosen)
 
     order = list(range(1, n))
-    coefs = {}
-    col_picks = {}
     copies_a, copies_b = {}, {}
+
+    def make_block(k):
+        p = lax.rem(me + k, n)
+        coefs = weights(row_ref[p], col_ref[p], index_ref[p], tile)
+        got = block_of(combine(loc, 0, rows, coefs), pick_cols(col_ref[p]), pick_rows(row_ref[p]))
+        block[k, 0] = got[:, :patch]
+        block[k, 1] = got[:, patch:]
+
+    def make_edge(slot, at, infos, tile_at, first_held, first_row):
+        shape = (MARGIN, MARGIN)
+        for p in range(n):
+            row_at, col_at = infos[0, p], infos[1, p]
+            coefs = weights(row_at, col_at, infos[2, p], tile_at)
+            shift = iota(shape, 1) - iota(shape, 0) + (first_held - first_row)
+            got = block_of(combine(loc, at, MARGIN, coefs), pick_cols(col_at), ones(shift == row_at))
+            edge[slot, p, 0] = got[:, :patch]
+            edge[slot, p, 1] = got[:, patch:]
+
     local[0].wait()
+    for k in order:
+        make_block(k)
+        copies_a[k] = remote(
+            block.at[k, :, pl.ds(MARGIN, middle), :],
+            recv_a.at[k - 1],
+            a_send.at[k - 1],
+            a_recv.at[k - 1],
+            {"beam": lax.rem(me + k, n)},
+        )
+        copies_a[k].start()
+
+    @pl.when(has_down)
+    def _():
+        up[0].wait_recv()
+        make_edge(0, rows - MARGIN, from_below, tile + 1, 0, 0)
+        down[2].start()
+
+    @pl.when(has_up)
+    def _():
+        down[0].wait_recv()
+        make_edge(1, 0, from_above, tile - 1, rows + MARGIN, patch - MARGIN)
+        up[2].start()
+
+    make_block(0)
+    local[1].wait()
+
+    @pl.when(has_down)
+    def _():
+        up[1].wait_recv()
+        up[2].wait_recv()
+
+    @pl.when(has_up)
+    def _():
+        down[1].wait_recv()
+        down[2].wait_recv()
+
     for k in order + [0]:
         p = lax.rem(me + k, n)
-        coefs[k] = weights(p)
-        col_picks[k] = pick_cols(p)
-        got = block_of(combine(loc, rows, coefs[k]), col_picks[k], pick_rows(p))
-        block[k, 0] = got[:, :patch]
-        block[k, 1] = got[:, patch:]
-        if k != 0:
-            copies_a[k] = remote(
-                block.at[k, :, pl.ds(MARGIN, middle), :],
-                recv_a.at[k - 1],
-                a_send.at[k - 1],
-                a_recv.at[k - 1],
-                {"beam": p},
-            )
-            copies_a[k].start()
-
-    local[1].wait()
-
-    @pl.when(has_down)
-    def _():
-        for copy in up:
-            copy.wait_recv()
-
-    @pl.when(has_up)
-    def _():
-        for copy in down:
-            copy.wait_recv()
-
-    for k in order + [0]:
-        p = lax.rem(me + k, n)
-        got = block_of(combine(halo, 2 * MARGIN, coefs[k]), col_picks[k], pick_halo(p, 2 * MARGIN))
         for c in range(2):
-            part = got[:, c * patch : (c + 1) * patch]
-            send_b[k, c, :MARGIN, :] = block[k, c, :MARGIN, :] + part[:MARGIN]
-            send_b[k, c, MARGIN:, :] = block[k, c, MARGIN + middle :, :] + part[MARGIN:]
+            send_b[k, c, :MARGIN, :] = block[k, c, :MARGIN, :] + halo[0, p, c]
+            send_b[k, c, MARGIN:, :] = block[k, c, MARGIN + middle :, :] + halo[1, p, c]
         if k != 0:
             copies_b[k] = remote(
                 send_b.at[k], recv_b.at[k - 1], b_send.at[k - 1], b_recv.at[k - 1], {"beam": p}
@@ -271,10 +299,11 @@
     tall = jnp.concatenate([ploc[...], phalo[...]], 0)
     high, low = split(tall)
     least = (tall - high.astype(jnp.float32) - low.astype(jnp.float32)).astype(jnp.bfloat16)
-    row_pick = jnp.concatenate([pick_rows(me), pick_halo(me, patch)], 1)
+    row_pick = jnp.concatenate([pick_rows(row_ref[me]), pick_halo(row_ref[me])], 1)
+    own_cols = pick_cols(col_ref[me])
     here = None
     for term in (least, low, high):
-        now = dot(row_pick, dot(term, col_picks[0]).astype(jnp.bfloat16))
+        now = dot(row_pick, dot(term, own_cols).astype(jnp.bfloat16))
         here = now if here is None else here + now
     here = here * SIGMA_SCALE
     trans[0] = jnp.cos(here)
@@ -364,6 +393,17 @@
     def _():
         for copy in down + [rim_down]:
             copy.wait_send()
+
+
+def hand_over(misfit, grad, misfit_out, grad_out, sem):
+    copies = [
+        pltpu.make_async_copy(misfit, misfit_out, sem.at[0]),
+        pltpu.make_async_copy(grad, grad_out, sem.at[1]),
+    ]
+    for copy in copies:
+        copy.start()
+    for copy in copies:
+        copy.wait()
 
 
 def shards(
@@ -400,7 +440,11 @@
         scratch_shapes=[
             pltpu.VMEM((beams, 2, rows, cols), f32),
             pltpu.VMEM((rows, cols), f32),
-            pltpu.VMEM((beams, 2, 2 * MARGIN, cols), f32),
+            pltpu.SMEM((3, n), jnp.int32),
+            pltpu.SMEM((3, n), jnp.int32),
+            pltpu.SMEM((3, n), jnp.int32),
+            pltpu.VMEM((2, n, 2, MARGIN, patch), f32),
+            pltpu.VMEM((2, n, 2, MARGIN, patch), f32),
             pltpu.VMEM((2 * MARGIN, cols), f32),
             pltpu.VMEM((patch, patch), f32),
             pltpu.VMEM((n, 2, patch, patch), f32),
@@ -413,8 +457,8 @@
             pltpu.VMEM((strip_rows, cols), f32),
             pltpu.VMEM((2, MARGIN, cols), f32),
             dma((3,)),
-            dma((4,)),
-            dma((4,)),
+            dma((6,)),
+            dma((6,)),
             dma((n - 1,)),
             dma((n - 1,)),
             dma((n - 1,)),
@@ -440,6 +484,17 @@
         potential,
         measured,
     )
+    misfit, grad = pl.pallas_call(
+        hand_over,
+        out_shape=(
+            jax.ShapeDtypeStruct((patch, patch), f32),
+            jax.ShapeDtypeStruct((rows, cols), f32),
+        ),
+        in_specs=[anywhere] * 2,
+        out_specs=(anywhere, anywhere),
+        scratch_shapes=[dma((2,))],
+        compiler_params=pltpu.CompilerParams(vmem_limit_bytes=56 * 1024 * 1024),
+    )(misfit, grad)
     return misfit[None, None], grad
 
 

time: 34.1 us -> 38 us (1.11)
  the two profiles are of different devices: /device:TPU:3 before, /device:TPU:1 now
where the time goes in v2:
time: 38 us; the launch traced here: 37.5 us
  Pallas kernels  36.9 us (97%)
  between operations  0.64 us (2%)
    pallas_call x1, Pallas kernels, shards(): pl.pallas_call(functools.partial(kernel, n, tiles), out_shape=(jax.ShapeD...  29.8 us
    pallas_call x1, Pallas kernels, shards(): pl.pallas_call(hand_over, out_shape=(jax.ShapeDtypeStruct((patch, patch),...  7.08 us

profile of v2, /device:TPU:1, one launch (start us, length us, event | category | flops | bytes accessed | tf_op | source)
XLA Modules:
  0.0 37.5 jit_solution(12199212262899436059)
XLA Ops:
  0.6 29.8 %shard_map.122 = (f32[128,128]{1,0:T(8,128)}, f32[128,256]{1,0:T(8,128)}) custom-call(s32[4]{0:T(128)} %bitcast.6, s32[4]{0:T(128)} %bitcast.7, s32[4]{0:T(128)} %bitcast.8, s32[2,4]{1,0:T(2,128)} %tilt_ref.1, f32[8,4]{1,0:T(8,128)} %bitcast.5, f32[2,128]{1,0:T(2,128)} %constant.6.clone.trig_ref, bf16[2,256,256]{2,1,0:T(8,128)(2,1)} %constant.7.clone.high_ref, ...), custom_call_target="tpu_custom_call" | custom-call | tf_op jit(solution)/shard_map/pallas_call | solution.py:432
  30.4 7.1 %shard_map.123 = (f32[128,128]{1,0:T(8,128)}, f32[128,256]{1,0:T(8,128)}) custom-call(f32[128,128]{1,0:T(8,128)} %get-tuple-element.6.misfit, f32[128,256]{1,0:T(8,128)} %get-tuple-element.7.grad), custom_call_target="tpu_custom_call" | custom-call | tf_op jit(solution)/shard_map/pallas_call | solution.py:487

commit v3 on v2

--- a/solution.py
+++ b/solution.py
@@ -64,8 +64,9 @@
     scat,
     pot,
     meas,
-    misfit_ref,
-    grad_ref,
+    power_ref,
+    core_ref,
+    extra_ref,
     loc,
     ploc,
     mine,
@@ -79,6 +80,8 @@
     send_b,
     recv_a,
     recv_b,
+    relay_a,
+    relay_b,
     trans,
     piece,
     recv_p,
@@ -95,6 +98,8 @@
     p_recv,
     rim_send,
     rim_recv,
+    relay_recv,
+    forward_send,
 ):
     me = lax.axis_index("beam")
     tile = lax.axis_index("tile")
@@ -248,17 +253,63 @@
             edge[slot, p, 0] = got[:, :patch]
             edge[slot, p, 1] = got[:, patch:]
 
+    def normal(k, src, dst, send_sem, recv_sem):
+        return remote(
+            src, dst.at[k - 1], send_sem.at[k - 1], recv_sem.at[k - 1], {"beam": lax.rem(me + k, n)}
+        )
+
+    def detour(k, src, relay, send_sem, relay_sem):
+        there = 1 if k == n - 1 else n - 2
+        return remote(src, relay, send_sem.at[k - 1], relay_sem, {"beam": there})
+
+    def ship(k, src, dst, relay, send_sem, recv_sem, relay_sem):
+        straight = normal(k, src, dst, send_sem, recv_sem)
+        if k in (1, n - 1):
+            at_end = me == (0 if k == n - 1 else n - 1)
+
+            @pl.when(at_end)
+            def _():
+                detour(k, src, relay, send_sem, relay_sem).start()
+
+            @pl.when(jnp.logical_not(at_end))
+            def _():
+                straight.start()
+        else:
+            straight.start()
+        return straight
+
+    def add_relayed(k, src, relay, send_sem, relay_sem):
+        for spot, where in ((n - 2, 1), (2, n - 2)):
+            if k == spot:
+
+                @pl.when(me == where)
+                def _():
+                    detour(1, src, relay, send_sem, relay_sem).wait_recv()
+                    src[...] += relay[...]
+
+    def take(k, copy):
+        if k in (1, n - 1):
+
+            @pl.when(me != (n - 1 if k == n - 1 else 0))
+            def _():
+                copy.wait_recv()
+        else:
+            copy.wait_recv()
+
+    for k, where in ((n - 1, n - 1), (1, 0)):
+
+        @pl.when(me == where)
+        def _():
+            recv_a[k - 1] = jnp.zeros(recv_a.shape[1:], jnp.float32)
+            recv_b[k - 1] = jnp.zeros(recv_b.shape[1:], jnp.float32)
+
     local[0].wait()
+    order = [n - 1, 1] + list(range(2, n - 1))
     for k in order:
         make_block(k)
-        copies_a[k] = remote(
-            block.at[k, :, pl.ds(MARGIN, middle), :],
-            recv_a.at[k - 1],
-            a_send.at[k - 1],
-            a_recv.at[k - 1],
-            {"beam": lax.rem(me + k, n)},
-        )
-        copies_a[k].start()
+        src = block.at[k, :, pl.ds(MARGIN, middle), :]
+        add_relayed(k, src, relay_a, a_send, relay_recv.at[0])
+        copies_a[k] = ship(k, src, recv_a, relay_a, a_send, a_recv, relay_recv.at[0])
 
     @pl.when(has_down)
     def _():
@@ -291,10 +342,9 @@
             send_b[k, c, :MARGIN, :] = block[k, c, :MARGIN, :] + halo[0, p, c]
             send_b[k, c, MARGIN:, :] = block[k, c, MARGIN + middle :, :] + halo[1, p, c]
         if k != 0:
-            copies_b[k] = remote(
-                send_b.at[k], recv_b.at[k - 1], b_send.at[k - 1], b_recv.at[k - 1], {"beam": p}
-            )
-            copies_b[k].start()
+            src = send_b.at[k]
+            add_relayed(k, src, relay_b, b_send, relay_recv.at[1])
+            copies_b[k] = ship(k, src, recv_b, relay_b, b_send, b_recv, relay_recv.at[1])
 
     tall = jnp.concatenate([ploc[...], phalo[...]], 0)
     high, low = split(tall)
@@ -310,8 +360,8 @@
     trans[1] = jnp.sin(here)
 
     for k in order:
-        copies_a[k].wait_recv()
-        copies_b[k].wait_recv()
+        take(k, copies_a[k])
+        take(k, copies_b[k])
     local[2].wait()
 
     parts = []
@@ -331,17 +381,27 @@
     back = (high_ref[1], low_ref[1])
     far = transform(jnp.concatenate([exit_re, exit_im], 0), back, ahead)
     far_re, far_im = far[:, :patch], far[:, patch:]
-    misfit = far_re * far_re + far_im * far_im - seen[...]
-    misfit_ref[...] = misfit
+    power = far_re * far_re + far_im * far_im
+    power_ref[...] = power
+    misfit = power - seen[...]
     turned = transform(jnp.concatenate([misfit * far_re, misfit * far_im], 0), ahead, back)
     piece[...] = SIGMA_SCALE * (exit_re * turned[:, patch:] - exit_im * turned[:, :patch])
 
     copies_p = {}
+    order = list(range(2, n - 1)) + [1, n - 1]
     for k in order:
-        copies_p[k] = remote(
-            piece, recv_p.at[k - 1], p_send.at[k - 1], p_recv.at[k - 1], {"beam": lax.rem(me + k, n)}
-        )
-        copies_p[k].start()
+        copies_p[k] = normal(k, piece, recv_p, p_send, p_recv)
+        if k in (1, n - 1):
+
+            @pl.when(me != (0 if k == n - 1 else n - 1))
+            def _():
+                copies_p[k].start()
+        else:
+            copies_p[k].start()
+    forwards = [
+        (n - 2, n - 2, remote(recv_p.at[n - 3], recv_p.at[n - 2], forward_send, p_recv.at[n - 2], {"beam": n - 1})),
+        (1, 2, remote(recv_p.at[1], recv_p.at[0], forward_send, p_recv.at[0], {"beam": 0})),
+    ]
 
     def place(value, p):
         shape = (patch, cols)
@@ -354,6 +414,9 @@
     strip[...] = place(piece[...], me)
     for k in order:
         copies_p[k].wait_recv()
+        for where, spot, copy in forwards:
+            if k == spot:
+                pl.when(me == where)(copy.start)
         strip[...] += place(recv_p[k - 1], lax.rem(me + n - k, n))
 
     rim_up = remote(strip.at[first, :], rims.at[1], rim_send.at[0], rim_recv.at[0], {"tile": tile - 1})
@@ -367,22 +430,28 @@
     def _():
         rim_down.start()
 
-    grad_ref[...] = strip[MARGIN : MARGIN + rows, :]
+    core_ref[...] = strip[MARGIN : MARGIN + rows, :]
+    extra_ref[...] = jnp.zeros(extra_ref.shape, jnp.float32)
 
     @pl.when(has_down)
     def _():
         rim_up.wait_recv()
-        grad_ref[rows - MARGIN :, :] += rims[1]
+        extra_ref[rows - MARGIN :, :] = rims[1]
 
     @pl.when(has_up)
     def _():
         rim_down.wait_recv()
-        grad_ref[:MARGIN, :] += rims[0]
+        extra_ref[:MARGIN, :] = rims[0]
 
     for k in order:
         copies_a[k].wait_send()
         copies_b[k].wait_send()
-        copies_p[k].wait_send()
+        if k in (1, n - 1):
+            pl.when(me != (0 if k == n - 1 else n - 1))(copies_p[k].wait_send)
+        else:
+            copies_p[k].wait_send()
+    for where, _, copy in forwards:
+        pl.when(me == where)(copy.wait_send)
 
     @pl.when(has_up)
     def _():
@@ -393,17 +462,6 @@
     def _():
         for copy in down + [rim_down]:
             copy.wait_send()
-
-
-def hand_over(misfit, grad, misfit_out, grad_out, sem):
-    copies = [
-        pltpu.make_async_copy(misfit, misfit_out, sem.at[0]),
-        pltpu.make_async_copy(grad, grad_out, sem.at[1]),
-    ]
-    for copy in copies:
-        copy.start()
-    for copy in copies:
-        copy.wait()
 
 
 def shards(
@@ -420,7 +478,7 @@
 ):
     beams, _, rows, cols = scattering.shape
     positions, patch = measured.shape[0], measured.shape[-1]
-    assert positions == n and patch & (patch - 1) == 0 and cols & (cols - 1) == 0
+    assert positions == n and n >= 4 and patch & (patch - 1) == 0 and cols & (cols - 1) == 0
     high, low, trig = tables(patch)
     f32 = jnp.float32
     middle = patch - 2 * MARGIN
@@ -429,14 +487,15 @@
     anywhere = pl.BlockSpec(memory_space=pl.ANY)
     strip_rows = rows + 2 * MARGIN
     dma = pltpu.SemaphoreType.DMA
-    misfit, grad = pl.pallas_call(
+    power, core, extra = pl.pallas_call(
         functools.partial(kernel, n, tiles),
         out_shape=(
             jax.ShapeDtypeStruct((patch, patch), f32),
             jax.ShapeDtypeStruct((rows, cols), f32),
+            jax.ShapeDtypeStruct((rows, cols), f32),
         ),
         in_specs=[smem] * 6 + [vmem] * 2 + [anywhere] * 3,
-        out_specs=(vmem, vmem),
+        out_specs=(vmem, vmem, vmem),
         scratch_shapes=[
             pltpu.VMEM((beams, 2, rows, cols), f32),
             pltpu.VMEM((rows, cols), f32),
@@ -451,6 +510,8 @@
             pltpu.VMEM((n, 2, 2 * MARGIN, patch), f32),
             pltpu.VMEM((n - 1, 2, middle, patch), f32),
             pltpu.VMEM((n - 1, 2, 2 * MARGIN, patch), f32),
+            pltpu.VMEM((2, middle, patch), f32),
+            pltpu.VMEM((2, 2 * MARGIN, patch), f32),
             pltpu.VMEM((2, patch, patch), f32),
             pltpu.VMEM((patch, patch), f32),
             pltpu.VMEM((n - 1, patch, patch), f32),
@@ -467,6 +528,8 @@
             dma((n - 1,)),
             dma((2,)),
             dma((2,)),
+            dma((2,)),
+            dma,
         ],
         compiler_params=pltpu.CompilerParams(
             collective_id=0, has_side_effects=True, vmem_limit_bytes=56 * 1024 * 1024
@@ -484,18 +547,8 @@
         potential,
         measured,
     )
-    misfit, grad = pl.pallas_call(
-        hand_over,
-        out_shape=(
-            jax.ShapeDtypeStruct((patch, patch), f32),
-            jax.ShapeDtypeStruct((rows, cols), f32),
-        ),
-        in_specs=[anywhere] * 2,
-        out_specs=(anywhere, anywhere),
-        scratch_shapes=[dma((2,))],
-        compiler_params=pltpu.CompilerParams(vmem_limit_bytes=56 * 1024 * 1024),
-    )(misfit, grad)
-    return misfit[None, None], grad
+    seen = lax.dynamic_index_in_dim(measured, lax.axis_index("beam"), 0, keepdims=True)
+    return power[None, None] - seen, core + extra
 
 
 def solution(mesh):

time: 38 us -> 38.4 us (1.011)
  other arithmetic: 0 us -> 3.13 us
  Pallas kernels: 36.9 us -> 34.5 us
    pallas_call x1 -> x0, Pallas kernels: 7.08 us -> none  [shards(): pl.pallas_call(hand_over, out_shape=(jax.ShapeDtypeStruct((patch, patch),...]
    pallas_call x1, Pallas kernels: 29.8 us -> 34.5 us  [shards(): pl.pallas_call(functools.partial(kernel, n, tiles), out_shape=(jax.ShapeD...]
    add x0 -> x1, other arithmetic: none -> 1.58 us  [shards(): return (power[None, None] - seen, core + extra)]
    sub x0 -> x1, other arithmetic: none -> 1.55 us  [shards(): return (power[None, None] - seen, core + extra)]
where the time goes in v3:
time: 38.4 us; the launch traced here: 38.3 us
  Pallas kernels  34.5 us (90%)
  other arithmetic  3.13 us (8%)
  between operations  0.65 us (2%)
    pallas_call x1, Pallas kernels, shards(): pl.pallas_call(functools.partial(kernel, n, tiles), out_shape=(jax.ShapeD...  34.5 us
    add x1, other arithmetic, shards(): return (power[None, None] - seen, core + extra)  1.58 us
    sub x1, other arithmetic, shards(): return (power[None, None] - seen, core + extra)  1.55 us

profile of v3, /device:TPU:1, one launch (start us, length us, event | category | flops | bytes accessed | tf_op | source)
XLA Modules:
  0.0 38.3 jit_solution(5169207669403160218)
XLA Ops:
  0.6 34.5 %shard_map.122 = (f32[128,128]{1,0:T(8,128)}, f32[128,256]{1,0:T(8,128)}, f32[128,256]{1,0:T(8,128)}) custom-call(s32[4]{0:T(128)} %bitcast.7, s32[4]{0:T(128)} %bitcast.8, s32[4]{0:T(128)} %bitcast.9, s32[2,4]{1,0:T(2,128)} %tilt_ref.1, f32[8,4]{1,0:T(8,128)} %bitcast.6, f32[2,128]{1,0:T(2,128)} %constant.17.clone.trig_ref, ...), custom_call_target="tpu_custom_call" | custom-call | tf_op jit(solution)/shard_map/pallas_call | solution.py:490
  35.1 0.0 copy-start
  35.1 1.6 %bitcast_subtract_fusion = f32[1,1,128,128]{3,2,1,0:T(8,128)} fusion(f32[128,128]{1,0:T(8,128)} %get-tuple-element.5, f32[4,1,128,128]{3,2,1,0:T(8,128)} %meas.1, s32[]{:T(128)S(6)} %select_n.4), kind=kLoop, calls=%fused_computation | loop fusion | flops 16384 | bytes 196612 | tf_op jit(solution)/shard_map/sub | solution.py:551
  36.7 0.0 copy-done
  36.7 1.6 %add.8 = f32[128,256]{1,0:T(8,128)} add(f32[128,256]{1,0:T(8,128)S(1)} %copy-done, f32[128,256]{1,0:T(8,128)} %get-tuple-element.7) | non-fusion elementwise | flops 32768 | bytes 393216 | tf_op jit(solution)/shard_map/add | solution.py:551
Async XLA Ops:
  35.1 1.6 %copy-start = (f32[128,256]{1,0:T(8,128)S(1)}, f32[128,256]{1,0:T(8,128)}, u32[]{:S(2)}) copy-start(f32[128,256]{1,0:T(8,128)} %get-tuple-element.6) | copy-start | bytes 393220

commit v4 on v2

--- a/solution.py
+++ b/solution.py
@@ -172,11 +172,17 @@
     @pl.when(tile == 0)
     def _():
         halo[0] = jnp.zeros(halo.shape[1:], jnp.float32)
+        for i in range(3):
+            for p in range(n):
+                from_above[i, p] = 0
         phalo[:MARGIN, :] = jnp.zeros((MARGIN, cols), jnp.float32)
 
     @pl.when(tile == tiles - 1)
     def _():
         halo[1] = jnp.zeros(halo.shape[1:], jnp.float32)
+        for i in range(3):
+            for p in range(n):
+                from_below[i, p] = 0
         phalo[MARGIN:, :] = jnp.zeros((MARGIN, cols), jnp.float32)
 
     def weights(row_at, col_at, picked, tile_at):
@@ -222,35 +228,37 @@
             total_im = now_im if total_im is None else total_im + now_im
         return jnp.concatenate(split(total_re) + split(total_im), 0)
 
-    def block_of(combined, col_pick, row_pick):
-        count = combined.shape[0] // 4
-        chosen = dot(combined, col_pick).astype(jnp.bfloat16)
-        chosen = jnp.concatenate([chosen[: 2 * count], chosen[2 * count :]], 1)
-        return dot(jnp.concatenate([row_pick, row_pick], 1), chosen)
+    def blocks_of(jobs):
+        sums = [combine(source, at, count, coefs) for source, at, count, coefs, _, _ in jobs]
+        chosen = [dot(total, job[4]).astype(jnp.bfloat16) for total, job in zip(sums, jobs)]
+        results = []
+        for pair, job in zip(chosen, jobs):
+            count = 2 * job[2]
+            pair = jnp.concatenate([pair[:count], pair[count:]], 1)
+            results.append(dot(jnp.concatenate([job[5], job[5]], 1), pair))
+        return results
+
+    def block_job(k):
+        p = lax.rem(me + k, n)
+        coefs = weights(row_ref[p], col_ref[p], index_ref[p], tile)
+        return loc, 0, rows, coefs, pick_cols(col_ref[p]), pick_rows(row_ref[p])
+
+    def edge_job(p, at, infos, tile_at, first_held, first_row):
+        shape = (MARGIN, MARGIN)
+        row_at, col_at = infos[0, p], infos[1, p]
+        coefs = weights(row_at, col_at, infos[2, p], tile_at)
+        shift = iota(shape, 1) - iota(shape, 0) + (first_held - first_row)
+        return loc, at, MARGIN, coefs, pick_cols(col_at), ones(shift == row_at)
+
+    def keep(ref, got):
+        ref[0] = got[:, :patch]
+        ref[1] = got[:, patch:]
 
     order = list(range(1, n))
     copies_a, copies_b = {}, {}
-
-    def make_block(k):
-        p = lax.rem(me + k, n)
-        coefs = weights(row_ref[p], col_ref[p], index_ref[p], tile)
-        got = block_of(combine(loc, 0, rows, coefs), pick_cols(col_ref[p]), pick_rows(row_ref[p]))
-        block[k, 0] = got[:, :patch]
-        block[k, 1] = got[:, patch:]
-
-    def make_edge(slot, at, infos, tile_at, first_held, first_row):
-        shape = (MARGIN, MARGIN)
-        for p in range(n):
-            row_at, col_at = infos[0, p], infos[1, p]
-            coefs = weights(row_at, col_at, infos[2, p], tile_at)
-            shift = iota(shape, 1) - iota(shape, 0) + (first_held - first_row)
-            got = block_of(combine(loc, at, MARGIN, coefs), pick_cols(col_at), ones(shift == row_at))
-            edge[slot, p, 0] = got[:, :patch]
-            edge[slot, p, 1] = got[:, patch:]
-
     local[0].wait()
-    for k in order:
-        make_block(k)
+    for k, got in zip(order, blocks_of([block_job(k) for k in order])):
+        keep(block.at[k], got)
         copies_a[k] = remote(
             block.at[k, :, pl.ds(MARGIN, middle), :],
             recv_a.at[k - 1],
@@ -263,16 +271,26 @@
     @pl.when(has_down)
     def _():
         up[0].wait_recv()
-        make_edge(0, rows - MARGIN, from_below, tile + 1, 0, 0)
+
+    @pl.when(has_up)
+    def _():
+        down[0].wait_recv()
+
+    spots = [(0, p) for p in range(n)] + [(1, p) for p in range(n)]
+    jobs = [edge_job(p, rows - MARGIN, from_below, tile + 1, 0, 0) for p in range(n)]
+    jobs += [edge_job(p, 0, from_above, tile - 1, rows + MARGIN, patch - MARGIN) for p in range(n)]
+    for (slot, p), got in zip(spots, blocks_of(jobs)):
+        keep(edge.at[slot, p], got)
+
+    @pl.when(has_down)
+    def _():
         down[2].start()
 
     @pl.when(has_up)
     def _():
-        down[0].wait_recv()
-        make_edge(1, 0, from_above, tile - 1, rows + MARGIN, patch - MARGIN)
         up[2].start()
 
-    make_block(0)
+    keep(block.at[0], blocks_of([block_job(0)])[0])
     local[1].wait()
 
     @pl.when(has_down)
@@ -393,17 +411,6 @@
     def _():
         for copy in down + [rim_down]:
             copy.wait_send()
-
-
-def hand_over(misfit, grad, misfit_out, grad_out, sem):
-    copies = [
-        pltpu.make_async_copy(misfit, misfit_out, sem.at[0]),
-        pltpu.make_async_copy(grad, grad_out, sem.at[1]),
-    ]
-    for copy in copies:
-        copy.start()
-    for copy in copies:
-        copy.wait()
 
 
 def shards(
@@ -484,17 +491,6 @@
         potential,
         measured,
     )
-    misfit, grad = pl.pallas_call(
-        hand_over,
-        out_shape=(
-            jax.ShapeDtypeStruct((patch, patch), f32),
-            jax.ShapeDtypeStruct((rows, cols), f32),
-        ),
-        in_specs=[anywhere] * 2,
-        out_specs=(anywhere, anywhere),
-        scratch_shapes=[dma((2,))],
-        compiler_params=pltpu.CompilerParams(vmem_limit_bytes=56 * 1024 * 1024),
-    )(misfit, grad)
     return misfit[None, None], grad
 
 

time: 38 us -> 34.1 us (0.90)
  Pallas kernels: 36.9 us -> 31.1 us
  local copies, waits for them, and re-layouts: 0 us -> 2.17 us
    pallas_call x1 -> x0, Pallas kernels: 7.08 us -> none  [shards(): pl.pallas_call(hand_over, out_shape=(jax.ShapeDtypeStruct((patch, patch),...]
    unnamed x0 -> x4, local copies, waits for them, and re-layouts: none -> 2.17 us
    pallas_call x1, Pallas kernels: 29.8 us -> 31.1 us  [shards(): pl.pallas_call(functools.partial(kernel, n, tiles), out_shape=(jax.ShapeD...]
where the time goes in v4:
time: 34.1 us; the launch traced here: 33.9 us
  Pallas kernels  31.1 us (91%)
  local copies, waits for them, and re-layouts  2.17 us (6%)
  between operations  0.65 us (2%)
    pallas_call x1, Pallas kernels, shards(): pl.pallas_call(functools.partial(kernel, n, tiles), out_shape=(jax.ShapeD...  31.1 us
    unnamed x4, local copies, waits for them, and re-layouts  2.17 us

profile of v4, /device:TPU:1, one launch (start us, length us, event | category | flops | bytes accessed | tf_op | source)
XLA Modules:
  0.0 33.9 jit_solution(2238634986976805087)
XLA Ops:
  0.6 31.1 %shard_map.122 = (f32[128,128]{1,0:T(8,128)}, f32[128,256]{1,0:T(8,128)}) custom-call(s32[4]{0:T(128)} %bitcast.7, s32[4]{0:T(128)} %bitcast.8, s32[4]{0:T(128)} %bitcast.9, s32[2,4]{1,0:T(2,128)} %tilt_ref.1, f32[8,4]{1,0:T(8,128)} %bitcast.6, f32[2,128]{1,0:T(2,128)} %constant.6.clone.trig_ref, bf16[2,256,256]{2,1,0:T(8,128)(2,1)} %constant.7.clone.high_ref, ...), custom_call_target="tpu_custom_call" | custom-call | tf_op jit(solution)/shard_map/pallas_call | solution.py:439
  31.7 0.0 copy-start
  31.7 1.5 %copy.18 = f32[1,1,128,128]{3,2,1,0:T(8,128)} copy(f32[1,1,128,128]{3,2,1,0:T(8,128)} %bitcast.5) | data formatting | bytes 131072
  33.3 0.0 copy-done
  33.3 0.7 %copy.19 = f32[128,256]{1,0:T(8,128)} copy(f32[128,256]{1,0:T(8,128)S(1)} %copy-done) | data formatting | bytes 262144
Async XLA Ops:
  31.7 1.5 %copy-start = (f32[128,256]{1,0:T(8,128)S(1)}, f32[128,256]{1,0:T(8,128)}, u32[]{:S(2)}) copy-start(f32[128,256]{1,0:T(8,128)} %get-tuple-element.9) | copy-start | bytes 393220

commit v5 on v1

--- a/solution.py
+++ b/solution.py
@@ -97,7 +97,7 @@
     beams = scat.shape[0]
     rows, cols = scat.shape[2], scat.shape[3]
     patch = seen.shape[-1]
-    middle = patch - 2 * MARGIN
+    early = patch - MARGIN
 
     local = [
         pltpu.make_async_copy(scat, loc, local_sem.at[0]),
@@ -190,18 +190,24 @@
         shape = (cols, patch)
         return ones(iota(shape, 0) - iota(shape, 1) == col_ref[p])
 
+    def turn_of(p, shape):
+        return jnp.where(jnp.full(shape, row_ref[p], jnp.int32) < MARGIN, MARGIN, 0)
+
     def pick_rows(p):
         shape = (patch, rows)
-        return ones(iota(shape, 1) - iota(shape, 0) == row_ref[p] - MARGIN)
-
-    def pick_halo(p, out_rows):
-        shape = (out_rows, 2 * MARGIN)
+        wanted = (iota(shape, 0) + turn_of(p, shape)) & (patch - 1)
+        return ones(iota(shape, 1) - wanted == row_ref[p] - MARGIN)
+
+    def pick_halo(p, first_row):
+        shape = (patch - first_row, 2 * MARGIN)
         held = iota(shape, 1)
         held = jnp.where(held < MARGIN, held, held + rows)
-        wanted = iota(shape, 0)
-        if out_rows < patch:
-            wanted = jnp.where(wanted < MARGIN, wanted, wanted + middle)
+        wanted = (iota(shape, 0) + first_row + turn_of(p, shape)) & (patch - 1)
         return ones(held - wanted == row_ref[p])
+
+    def unturn(value, p):
+        turned = jnp.concatenate([value[early:], value[:early]], 0)
+        return jnp.where(turn_of(p, value.shape) > 0, turned, value)
 
     def combine(source, count, coefs):
         total_re = total_im = None
@@ -235,7 +241,7 @@
         block[k, 1] = got[:, patch:]
         if k != 0:
             copies_a[k] = remote(
-                block.at[k, :, pl.ds(MARGIN, middle), :],
+                block.at[k, :, pl.ds(0, early), :],
                 recv_a.at[k - 1],
                 a_send.at[k - 1],
                 a_recv.at[k - 1],
@@ -255,13 +261,12 @@
         for copy in down:
             copy.wait_recv()
 
-    for k in order + [0]:
+    jobs = [(combine(halo, 2 * MARGIN, coefs[k]), pick_halo(lax.rem(me + k, n), early)) for k in order + [0]]
+    for k, (combined, row_pick) in zip(order + [0], jobs):
         p = lax.rem(me + k, n)
-        got = block_of(combine(halo, 2 * MARGIN, coefs[k]), col_picks[k], pick_halo(p, 2 * MARGIN))
+        got = block_of(combined, col_picks[k], row_pick)
         for c in range(2):
-            part = got[:, c * patch : (c + 1) * patch]
-            send_b[k, c, :MARGIN, :] = block[k, c, :MARGIN, :] + part[:MARGIN]
-            send_b[k, c, MARGIN:, :] = block[k, c, MARGIN + middle :, :] + part[MARGIN:]
+            send_b[k, c] = block[k, c, early:, :] + got[:, c * patch : (c + 1) * patch]
         if k != 0:
             copies_b[k] = remote(
                 send_b.at[k], recv_b.at[k - 1], b_send.at[k - 1], b_recv.at[k - 1], {"beam": p}
@@ -271,12 +276,12 @@
     tall = jnp.concatenate([ploc[...], phalo[...]], 0)
     high, low = split(tall)
     least = (tall - high.astype(jnp.float32) - low.astype(jnp.float32)).astype(jnp.bfloat16)
-    row_pick = jnp.concatenate([pick_rows(me), pick_halo(me, patch)], 1)
+    row_pick = jnp.concatenate([pick_rows(me), pick_halo(me, 0)], 1)
     here = None
     for term in (least, low, high):
         now = dot(row_pick, dot(term, col_picks[0]).astype(jnp.bfloat16))
         here = now if here is None else here + now
-    here = here * SIGMA_SCALE
+    here = unturn(here, me) * SIGMA_SCALE
     trans[0] = jnp.cos(here)
     trans[1] = jnp.sin(here)
 
@@ -287,14 +292,12 @@
 
     parts = []
     for c in range(2):
-        mid = block[0, c, MARGIN : MARGIN + middle, :]
-        head = send_b[0, c, :MARGIN, :]
-        tail = send_b[0, c, MARGIN:, :]
+        body = block[0, c, :early, :]
+        rest = send_b[0, c]
         for k in order:
-            mid += recv_a[k - 1, c]
-            head += recv_b[k - 1, c, :MARGIN, :]
-            tail += recv_b[k - 1, c, MARGIN:, :]
-        parts.append(jnp.concatenate([head, mid, tail], 0))
+            body += recv_a[k - 1, c]
+            rest += recv_b[k - 1, c]
+        parts.append(unturn(jnp.concatenate([body, rest], 0), me))
     wave_re, wave_im = parts
     exit_re = trans[0] * wave_re - trans[1] * wave_im
     exit_im = trans[0] * wave_im + trans[1] * wave_re
@@ -314,18 +317,22 @@
         )
         copies_p[k].start()
 
-    def place(value, p):
+    def spots(p):
         shape = (patch, cols)
         col_place = ones(iota(shape, 1) - iota(shape, 0) == col_ref[p])
         shape = (rows + 2 * MARGIN, patch)
         row_place = ones(iota(shape, 0) - iota(shape, 1) == row_ref[p])
-        moved = dot(jnp.concatenate(split(value), 0), col_place).astype(jnp.bfloat16)
-        return dot(jnp.concatenate([row_place, row_place], 1), moved)
-
-    strip[...] = place(piece[...], me)
+        return col_place, jnp.concatenate([row_place, row_place], 1)
+
+    def place(value, spot):
+        moved = dot(jnp.concatenate(split(value), 0), spot[0]).astype(jnp.bfloat16)
+        return dot(spot[1], moved)
+
+    places = [spots(lax.rem(me + n - k, n)) for k in range(n)]
+    strip[...] = place(piece[...], places[0])
     for k in order:
         copies_p[k].wait_recv()
-        strip[...] += place(recv_p[k - 1], lax.rem(me + n - k, n))
+        strip[...] += place(recv_p[k - 1], places[k])
 
     rim_up = remote(strip.at[first, :], rims.at[1], rim_send.at[0], rim_recv.at[0], {"tile": tile - 1})
     rim_down = remote(strip.at[below, :], rims.at[0], rim_send.at[1], rim_recv.at[1], {"tile": tile + 1})
@@ -383,7 +390,7 @@
     assert positions == n and patch & (patch - 1) == 0 and cols & (cols - 1) == 0
     high, low, trig = tables(patch)
     f32 = jnp.float32
-    middle = patch - 2 * MARGIN
+    early = patch - MARGIN
     smem = pl.BlockSpec(memory_space=pltpu.SMEM)
     vmem = pl.BlockSpec(memory_space=pltpu.VMEM)
     anywhere = pl.BlockSpec(memory_space=pl.ANY)
@@ -404,9 +411,9 @@
             pltpu.VMEM((2 * MARGIN, cols), f32),
             pltpu.VMEM((patch, patch), f32),
             pltpu.VMEM((n, 2, patch, patch), f32),
-            pltpu.VMEM((n, 2, 2 * MARGIN, patch), f32),
-            pltpu.VMEM((n - 1, 2, middle, patch), f32),
-            pltpu.VMEM((n - 1, 2, 2 * MARGIN, patch), f32),
+            pltpu.VMEM((n, 2, MARGIN, patch), f32),
+            pltpu.VMEM((n - 1, 2, patch - MARGIN, patch), f32),
+            pltpu.VMEM((n - 1, 2, MARGIN, patch), f32),
             pltpu.VMEM((2, patch, patch), f32),
             pltpu.VMEM((patch, patch), f32),
             pltpu.VMEM((n - 1, patch, patch), f32),

time: 34.1 us -> 32.6 us (0.956)
  the two profiles are of different devices: /device:TPU:3 before, /device:TPU:1 now
where the time goes in v5:
time: 32.6 us; the launch traced here: 32.5 us
  Pallas kernels  29.7 us (91%)
  local copies, waits for them, and re-layouts  2.17 us (7%)
  between operations  0.65 us (2%)
    pallas_call x1, Pallas kernels, shards(): pl.pallas_call(functools.partial(kernel, n, tiles), out_shape=(jax.ShapeD...  29.7 us
    unnamed x4, local copies, waits for them, and re-layouts  2.17 us

profile of v5, /device:TPU:1, one launch (start us, length us, event | category | flops | bytes accessed | tf_op | source)
XLA Modules:
  0.0 32.5 jit_solution(18128683539611093132)
XLA Ops:
  0.6 29.7 %shard_map.122 = (f32[128,128]{1,0:T(8,128)}, f32[128,256]{1,0:T(8,128)}) custom-call(s32[4]{0:T(128)} %bitcast.7, s32[4]{0:T(128)} %bitcast.8, s32[4]{0:T(128)} %bitcast.9, s32[2,4]{1,0:T(2,128)} %tilt_ref.1, f32[8,4]{1,0:T(8,128)} %bitcast.6, f32[2,128]{1,0:T(2,128)} %constant.6.clone.trig_ref, bf16[2,256,256]{2,1,0:T(8,128)(2,1)} %constant.7.clone.high_ref, ...), custom_call_target="tpu_custom_call" | custom-call | tf_op jit(solution)/shard_map/pallas_call | solution.py:399
  30.3 0.0 copy-start
  30.3 1.5 %copy.18 = f32[1,1,128,128]{3,2,1,0:T(8,128)} copy(f32[1,1,128,128]{3,2,1,0:T(8,128)} %bitcast.5) | data formatting | bytes 131072
  31.8 0.0 copy-done
  31.8 0.7 %copy.19 = f32[128,256]{1,0:T(8,128)} copy(f32[128,256]{1,0:T(8,128)S(1)} %copy-done) | data formatting | bytes 262144
Async XLA Ops:
  30.3 1.5 %copy-start = (f32[128,256]{1,0:T(8,128)S(1)}, f32[128,256]{1,0:T(8,128)}, u32[]{:S(2)}) copy-start(f32[128,256]{1,0:T(8,128)} %get-tuple-element.9) | copy-start | bytes 393220

commit v6 on v5

--- a/solution.py
+++ b/solution.py
@@ -123,6 +123,80 @@
     def _():
         pl.semaphore_signal(barrier, inc=1, device_id={"tile": tile + 1}, device_id_type=MESH)
 
+    def weights(p):
+        corner = row_ref[p] + tile * rows - MARGIN
+        picked = index_ref[p]
+        result = []
+        for b in range(beams):
+            turn = (tilt_ref[0, b] * corner + tilt_ref[1, b] * col_ref[p]) & (patch - 1)
+            cos, sin = trig_ref[0, turn], trig_ref[1, turn]
+            q_re = coef_ref[picked, b]
+            q_im = coef_ref[picked + coef_ref.shape[0] // 2, b]
+            result.append((q_re * cos + q_im * sin, q_im * cos - q_re * sin))
+        return result
+
+    def iota(shape, axis):
+        return lax.broadcasted_iota(jnp.int32, shape, axis)
+
+    def ones(mask):
+        return jnp.where(mask, 1.0, 0.0).astype(jnp.bfloat16)
+
+    def pick_cols(p):
+        shape = (cols, patch)
+        return ones(iota(shape, 0) - iota(shape, 1) == col_ref[p])
+
+    def turn_of(p, shape):
+        return jnp.where(jnp.full(shape, row_ref[p], jnp.int32) < MARGIN, MARGIN, 0)
+
+    def pick_rows(p):
+        shape = (patch, rows)
+        wanted = (iota(shape, 0) + turn_of(p, shape)) & (patch - 1)
+        return ones(iota(shape, 1) - wanted == row_ref[p] - MARGIN)
+
+    def pick_halo(p, first_row):
+        shape = (patch - first_row, 2 * MARGIN)
+        held = iota(shape, 1)
+        held = jnp.where(held < MARGIN, held, held + rows)
+        wanted = (iota(shape, 0) + first_row + turn_of(p, shape)) & (patch - 1)
+        return ones(held - wanted == row_ref[p])
+
+    def unturn(value, p):
+        turned = jnp.concatenate([value[early:], value[:early]], 0)
+        return jnp.where(turn_of(p, value.shape) > 0, turned, value)
+
+    def combine(source, count, coefs):
+        total_re = total_im = None
+        for b in range(beams):
+            re = source[b, 0, :count, :]
+            im = source[b, 1, :count, :]
+            c_re, c_im = coefs[b]
+            now_re = c_re * re - c_im * im
+            now_im = c_re * im + c_im * re
+            total_re = now_re if total_re is None else total_re + now_re
+            total_im = now_im if total_im is None else total_im + now_im
+        return jnp.concatenate(split(total_re) + split(total_im), 0)
+
+    def block_of(combined, col_pick, row_pick):
+        count = combined.shape[0] // 4
+        chosen = dot(combined, col_pick).astype(jnp.bfloat16)
+        chosen = jnp.concatenate([chosen[: 2 * count], chosen[2 * count :]], 1)
+        return dot(jnp.concatenate([row_pick, row_pick], 1), chosen)
+
+    order = sorted(range(1, n), key=lambda k: abs(2 * k - n))
+    coefs = {}
+    col_picks = {}
+
+    def make_block(k):
+        p = lax.rem(me + k, n)
+        coefs[k] = weights(p)
+        col_picks[k] = pick_cols(p)
+        got = block_of(combine(loc, rows, coefs[k]), col_picks[k], pick_rows(p))
+        block[k, 0] = got[:, :patch]
+        block[k, 1] = got[:, patch:]
+
+    local[0].wait()
+    make_block(order[0])
+
     pl.semaphore_wait(barrier, n - 1 + has_up.astype(jnp.int32) + has_down.astype(jnp.int32))
 
     def remote(src, dst, send_sem, recv_sem, where):
@@ -168,77 +242,11 @@
         halo[:, :, MARGIN:, :] = jnp.zeros((beams, 2, MARGIN, cols), jnp.float32)
         phalo[MARGIN:, :] = jnp.zeros((MARGIN, cols), jnp.float32)
 
-    def weights(p):
-        corner = row_ref[p] + tile * rows - MARGIN
-        picked = index_ref[p]
-        result = []
-        for b in range(beams):
-            turn = (tilt_ref[0, b] * corner + tilt_ref[1, b] * col_ref[p]) & (patch - 1)
-            cos, sin = trig_ref[0, turn], trig_ref[1, turn]
-            q_re = coef_ref[picked, b]
-            q_im = coef_ref[picked + coef_ref.shape[0] // 2, b]
-            result.append((q_re * cos + q_im * sin, q_im * cos - q_re * sin))
-        return result
-
-    def iota(shape, axis):
-        return lax.broadcasted_iota(jnp.int32, shape, axis)
-
-    def ones(mask):
-        return jnp.where(mask, 1.0, 0.0).astype(jnp.bfloat16)
-
-    def pick_cols(p):
-        shape = (cols, patch)
-        return ones(iota(shape, 0) - iota(shape, 1) == col_ref[p])
-
-    def turn_of(p, shape):
-        return jnp.where(jnp.full(shape, row_ref[p], jnp.int32) < MARGIN, MARGIN, 0)
-
-    def pick_rows(p):
-        shape = (patch, rows)
-        wanted = (iota(shape, 0) + turn_of(p, shape)) & (patch - 1)
-        return ones(iota(shape, 1) - wanted == row_ref[p] - MARGIN)
-
-    def pick_halo(p, first_row):
-        shape = (patch - first_row, 2 * MARGIN)
-        held = iota(shape, 1)
-        held = jnp.where(held < MARGIN, held, held + rows)
-        wanted = (iota(shape, 0) + first_row + turn_of(p, shape)) & (patch - 1)
-        return ones(held - wanted == row_ref[p])
-
-    def unturn(value, p):
-        turned = jnp.concatenate([value[early:], value[:early]], 0)
-        return jnp.where(turn_of(p, value.shape) > 0, turned, value)
-
-    def combine(source, count, coefs):
-        total_re = total_im = None
-        for b in range(beams):
-            re = source[b, 0, :count, :]
-            im = source[b, 1, :count, :]
-            c_re, c_im = coefs[b]
-            now_re = c_re * re - c_im * im
-            now_im = c_re * im + c_im * re
-            total_re = now_re if total_re is None else total_re + now_re
-            total_im = now_im if total_im is None else total_im + now_im
-        return jnp.concatenate(split(total_re) + split(total_im), 0)
-
-    def block_of(combined, col_pick, row_pick):
-        count = combined.shape[0] // 4
-        chosen = dot(combined, col_pick).astype(jnp.bfloat16)
-        chosen = jnp.concatenate([chosen[: 2 * count], chosen[2 * count :]], 1)
-        return dot(jnp.concatenate([row_pick, row_pick], 1), chosen)
-
-    order = list(range(1, n))
-    coefs = {}
-    col_picks = {}
     copies_a, copies_b = {}, {}
-    local[0].wait()
     for k in order + [0]:
+        if k != order[0]:
+            make_block(k)
         p = lax.rem(me + k, n)
-        coefs[k] = weights(p)
-        col_picks[k] = pick_cols(p)
-        got = block_of(combine(loc, rows, coefs[k]), col_picks[k], pick_rows(p))
-        block[k, 0] = got[:, :patch]
-        block[k, 1] = got[:, patch:]
         if k != 0:
             copies_a[k] = remote(
                 block.at[k, :, pl.ds(0, early), :],
@@ -324,15 +332,24 @@
         row_place = ones(iota(shape, 0) - iota(shape, 1) == row_ref[p])
         return col_place, jnp.concatenate([row_place, row_place], 1)
 
-    def place(value, spot):
-        moved = dot(jnp.concatenate(split(value), 0), spot[0]).astype(jnp.bfloat16)
-        return dot(spot[1], moved)
+    def move(value, spot):
+        return dot(jnp.concatenate(split(value), 0), spot[0]).astype(jnp.bfloat16)
 
     places = [spots(lax.rem(me + n - k, n)) for k in range(n)]
-    strip[...] = place(piece[...], places[0])
-    for k in order:
+    strip[...] = dot(places[0][1], move(piece[...], places[0]))
+    for k in order[: n - 3]:
         copies_p[k].wait_recv()
-        strip[...] += place(recv_p[k - 1], places[k])
+        strip[...] += dot(places[k][1], move(recv_p[k - 1], places[k]))
+    final = order[n - 3 :]
+    for k in final:
+        copies_p[k].wait_recv()
+    moved = jnp.concatenate([move(recv_p[k - 1], places[k]) for k in final], 0)
+    final_rows = jnp.concatenate([places[k][1] for k in final], 1)
+    lower = rows + MARGIN
+    rim_rows = jnp.concatenate([final_rows[:MARGIN], final_rows[lower:]], 0)
+    rim = dot(rim_rows, moved)
+    strip[:MARGIN, :] += rim[:MARGIN]
+    strip[lower:, :] += rim[MARGIN:]
 
     rim_up = remote(strip.at[first, :], rims.at[1], rim_send.at[0], rim_recv.at[0], {"tile": tile - 1})
     rim_down = remote(strip.at[below, :], rims.at[0], rim_send.at[1], rim_recv.at[1], {"tile": tile + 1})
@@ -345,7 +362,7 @@
     def _():
         rim_down.start()
 
-    grad_ref[...] = strip[MARGIN : MARGIN + rows, :]
+    grad_ref[...] = strip[MARGIN:lower, :] + dot(final_rows[MARGIN:lower], moved)
 
     @pl.when(has_down)
     def _():

time: 32.6 us -> 33.5 us (1.028)
  Pallas kernels: 29.7 us -> 30.5 us
    pallas_call x1, Pallas kernels: 29.7 us -> 30.5 us  [shards(): pl.pallas_call(functools.partial(kernel, n, tiles), out_shape=(jax.ShapeD...]
where the time goes in v6:
time: 33.5 us; the launch traced here: 33.3 us
  Pallas kernels  30.5 us (91%)
  local copies, waits for them, and re-layouts  2.17 us (6%)
  between operations  0.65 us (2%)
    pallas_call x1, Pallas kernels, shards(): pl.pallas_call(functools.partial(kernel, n, tiles), out_shape=(jax.ShapeD...  30.5 us
    unnamed x4, local copies, waits for them, and re-layouts  2.17 us

profile of v6, /device:TPU:1, one launch (start us, length us, event | category | flops | bytes accessed | tf_op | source)
XLA Modules:
  0.0 33.3 jit_solution(6779865953646129220)
XLA Ops:
  0.6 30.5 %shard_map.122 = (f32[128,128]{1,0:T(8,128)}, f32[128,256]{1,0:T(8,128)}) custom-call(s32[4]{0:T(128)} %bitcast.7, s32[4]{0:T(128)} %bitcast.8, s32[4]{0:T(128)} %bitcast.9, s32[2,4]{1,0:T(2,128)} %tilt_ref.1, f32[8,4]{1,0:T(8,128)} %bitcast.6, f32[2,128]{1,0:T(2,128)} %constant.6.clone.trig_ref, bf16[2,256,256]{2,1,0:T(8,128)(2,1)} %constant.7.clone.high_ref, ...), custom_call_target="tpu_custom_call" | custom-call | tf_op jit(solution)/shard_map/pallas_call | solution.py:416
  31.1 0.0 copy-start
  31.1 1.5 %copy.18 = f32[1,1,128,128]{3,2,1,0:T(8,128)} copy(f32[1,1,128,128]{3,2,1,0:T(8,128)} %bitcast.5) | data formatting | bytes 131072
  32.7 0.0 copy-done
  32.7 0.7 %copy.19 = f32[128,256]{1,0:T(8,128)} copy(f32[128,256]{1,0:T(8,128)S(1)} %copy-done) | data formatting | bytes 262144
Async XLA Ops:
  31.1 1.5 %copy-start = (f32[128,256]{1,0:T(8,128)S(1)}, f32[128,256]{1,0:T(8,128)}, u32[]{:S(2)}) copy-start(f32[128,256]{1,0:T(8,128)} %get-tuple-element.9) | copy-start | bytes 393220

commit v7 on v6

--- a/solution.py
+++ b/solution.py
@@ -66,8 +66,6 @@
     meas,
     misfit_ref,
     grad_ref,
-    loc,
-    ploc,
     halo,
     phalo,
     seen,
@@ -100,9 +98,7 @@
     early = patch - MARGIN
 
     local = [
-        pltpu.make_async_copy(scat, loc, local_sem.at[0]),
-        pltpu.make_async_copy(pot, ploc, local_sem.at[1]),
-        pltpu.make_async_copy(meas.at[me, 0], seen, local_sem.at[2]),
+        pltpu.make_async_copy(meas.at[me, 0], seen, local_sem.at[0]),
     ]
     for copy in local:
         copy.start()
@@ -190,11 +186,10 @@
         p = lax.rem(me + k, n)
         coefs[k] = weights(p)
         col_picks[k] = pick_cols(p)
-        got = block_of(combine(loc, rows, coefs[k]), col_picks[k], pick_rows(p))
+        got = block_of(combine(scat, rows, coefs[k]), col_picks[k], pick_rows(p))
         block[k, 0] = got[:, :patch]
         block[k, 1] = got[:, patch:]
 
-    local[0].wait()
     make_block(order[0])
 
     pl.semaphore_wait(barrier, n - 1 + has_up.astype(jnp.int32) + has_down.astype(jnp.int32))
@@ -257,7 +252,6 @@
             )
             copies_a[k].start()
 
-    local[1].wait()
 
     @pl.when(has_down)
     def _():
@@ -281,7 +275,7 @@
             )
             copies_b[k].start()
 
-    tall = jnp.concatenate([ploc[...], phalo[...]], 0)
+    tall = jnp.concatenate([pot[...], phalo[...]], 0)
     high, low = split(tall)
     least = (tall - high.astype(jnp.float32) - low.astype(jnp.float32)).astype(jnp.bfloat16)
     row_pick = jnp.concatenate([pick_rows(me), pick_halo(me, 0)], 1)
@@ -296,7 +290,7 @@
     for k in order:
         copies_a[k].wait_recv()
         copies_b[k].wait_recv()
-    local[2].wait()
+    local[0].wait()
 
     parts = []
     for c in range(2):
@@ -337,14 +331,14 @@
 
     places = [spots(lax.rem(me + n - k, n)) for k in range(n)]
     strip[...] = dot(places[0][1], move(piece[...], places[0]))
-    for k in order[: n - 3]:
+    near, far_k = order[1:], order[0]
+    for k in near:
         copies_p[k].wait_recv()
-        strip[...] += dot(places[k][1], move(recv_p[k - 1], places[k]))
-    final = order[n - 3 :]
-    for k in final:
-        copies_p[k].wait_recv()
-    moved = jnp.concatenate([move(recv_p[k - 1], places[k]) for k in final], 0)
-    final_rows = jnp.concatenate([places[k][1] for k in final], 1)
+    moved = jnp.concatenate([move(recv_p[k - 1], places[k]) for k in near], 0)
+    strip[...] += dot(jnp.concatenate([places[k][1] for k in near], 1), moved)
+    copies_p[far_k].wait_recv()
+    moved = move(recv_p[far_k - 1], places[far_k])
+    final_rows = places[far_k][1]
     lower = rows + MARGIN
     rim_rows = jnp.concatenate([final_rows[:MARGIN], final_rows[lower:]], 0)
     rim = dot(rim_rows, moved)
@@ -419,11 +413,9 @@
             jax.ShapeDtypeStruct((patch, patch), f32),
             jax.ShapeDtypeStruct((rows, cols), f32),
         ),
-        in_specs=[smem] * 6 + [vmem] * 2 + [anywhere] * 3,
+        in_specs=[smem] * 6 + [vmem] * 4 + [anywhere],
         out_specs=(vmem, vmem),
         scratch_shapes=[
-            pltpu.VMEM((beams, 2, rows, cols), f32),
-            pltpu.VMEM((rows, cols), f32),
             pltpu.VMEM((beams, 2, 2 * MARGIN, cols), f32),
             pltpu.VMEM((2 * MARGIN, cols), f32),
             pltpu.VMEM((patch, patch), f32),
@@ -436,7 +428,7 @@
             pltpu.VMEM((n - 1, patch, patch), f32),
             pltpu.VMEM((strip_rows, cols), f32),
             pltpu.VMEM((2, MARGIN, cols), f32),
-            dma((3,)),
+            dma((1,)),
             dma((4,)),
             dma((4,)),
             dma((n - 1,)),
@@ -449,7 +441,7 @@
             dma((2,)),
         ],
         compiler_params=pltpu.CompilerParams(
-            collective_id=0, has_side_effects=True, vmem_limit_bytes=56 * 1024 * 1024
+            collective_id=0, has_side_effects=True, vmem_limit_bytes=12 * 1024 * 1024
         ),
     )(
         row_offset[:, 0],

time: 33.5 us -> 37 us (1.10)
  local copies, waits for them, and re-layouts: 2.17 us -> 6.96 us
  Pallas kernels: 30.5 us -> 29 us
    unnamed x4 -> x24, local copies, waits for them, and re-layouts: 2.17 us -> 6.96 us
    pallas_call x1, Pallas kernels: 30.5 us -> 29 us  [shards(): pl.pallas_call(functools.partial(kernel, n, tiles), out_shape=(jax.ShapeD...]
where the time goes in v7:
time: 37 us; the launch traced here: 36.7 us
  Pallas kernels  29 us (78%)
  local copies, waits for them, and re-layouts  6.96 us (19%)
  between operations  0.7 us (2%)
    pallas_call x1, Pallas kernels, shards(): pl.pallas_call(functools.partial(kernel, n, tiles), out_shape=(jax.ShapeD...  29 us
    unnamed x24, local copies, waits for them, and re-layouts  6.96 us

profile of v7, /device:TPU:1, one launch (start us, length us, event | category | flops | bytes accessed | tf_op | source)
XLA Modules:
  0.0 36.7 jit_solution(15386969331611766530)
XLA Ops:
  0.6 0.0 copy-start.5
  0.6 0.0 copy-start.7
  0.7 0.0 copy-start.9
  0.7 0.0 copy-start.10
  0.7 0.0 copy-start.6
  0.7 0.0 copy-start.8
  0.7 0.6 %copy-done.5 = f32[2,4,4]{2,1,0:T(4,128)S(1)} copy-done((f32[2,4,4]{2,1,0:T(4,128)S(1)}, f32[2,4,4]{2,1,0:T(4,128)}, u32[]{:S(2)}) %copy-start.5) | copy-done | bytes 152
  1.3 0.0 copy-done.7
  1.3 0.0 copy-done.9
  1.3 0.0 copy-done.10
  1.3 0.0 copy-done.6
  1.4 0.0 copy-done.8
  1.4 0.0 copy-start
  1.4 1.2 %copy-done = f32[4,2,128,256]{3,2,1,0:T(8,128)S(1)} copy-done((f32[4,2,128,256]{3,2,1,0:T(8,128)S(1)}, f32[4,2,128,256]{3,2,1,0:T(8,128)}, u32[]{:S(2)}) %copy-start) | copy-done | bytes 1048600
  2.6 0.0 copy-start.1
  2.6 0.9 %copy-done.1 = f32[4,1,128,128]{3,2,1,0:T(8,128)S(1)} copy-done((f32[4,1,128,128]{3,2,1,0:T(8,128)S(1)}, f32[4,1,128,128]{3,2,1,0:T(8,128)}, u32[]{:S(2)}) %copy-start.1) | copy-done | bytes 262168
  3.6 0.0 copy-start.2
  3.6 0.9 %copy-done.2 = bf16[2,256,256]{2,1,0:T(8,128)(2,1)S(1)} copy-done((bf16[2,256,256]{2,1,0:T(8,128)(2,1)S(1)}, bf16[2,256,256]{2,1,0:T(8,128)(2,1)}, u32[]{:S(2)}) %copy-start.2) | copy-done | bytes 262168
  4.5 0.0 copy-start.3
  4.5 0.9 %copy-done.3 = bf16[2,256,256]{2,1,0:T(8,128)(2,1)S(1)} copy-done((bf16[2,256,256]{2,1,0:T(8,128)(2,1)S(1)}, bf16[2,256,256]{2,1,0:T(8,128)(2,1)}, u32[]{:S(2)}) %copy-start.3) | copy-done | bytes 262168
  5.5 0.9 %copy-done.4 = f32[128,256]{1,0:T(8,128)S(1)} copy-done((f32[128,256]{1,0:T(8,128)S(1)}, f32[128,256]{1,0:T(8,128)}, u32[]{:S(2)}) %copy-start.4) | copy-done | bytes 131096
  6.4 29.0 %shard_map.122 = (f32[128,128]{1,0:T(8,128)S(1)}, f32[128,256]{1,0:T(8,128)S(1)}) custom-call(s32[4]{0:T(128)S(1)} %bitcast.7, s32[4]{0:T(128)S(1)} %bitcast.8, s32[4]{0:T(128)S(1)} %bitcast.9, s32[2,4]{1,0:T(2,128)S(1)} %copy-done.6, f32[8,4]{1,0:T(8,128)S(1)} %bitcast.6, f32[2,128]{1,0:T(2,128)S(1)} %copy-done.7, bf16[2,256,256]{2,1,0:T(8,128)(2,1)S(1)} %copy-done.3, ...), custom_call_target="tpu_custom_call" | custom-call | tf_op jit(solution)/shard_map/pallas_call | solution.py:410
  35.4 0.6 %copy.18 = f32[1,1,128,128]{3,2,1,0:T(8,128)} copy(f32[1,1,128,128]{3,2,1,0:T(8,128)S(1)} %bitcast.5) | data formatting | bytes 131072
  36.0 0.7 %copy.19 = f32[128,256]{1,0:T(8,128)} copy(f32[128,256]{1,0:T(8,128)S(1)} %get-tuple-element.9) | data formatting | bytes 262144
  (1 shorter events, 0.0 us)
Async XLA Ops:
  0.6 0.7 %copy-start.5 = (f32[2,4,4]{2,1,0:T(4,128)S(1)}, f32[2,4,4]{2,1,0:T(4,128)}, u32[]{:S(2)}) copy-start(f32[2,4,4]{2,1,0:T(4,128)} %param.17) | copy-start | bytes 388
  0.6 0.7 %copy-start.7 = (f32[2,128]{1,0:T(2,128)S(1)}, f32[2,128]{1,0:T(2,128)}, u32[]{:S(2)}) copy-start(f32[2,128]{1,0:T(2,128)} %constant.6.clone.trig_ref) | copy-start | bytes 3076
  0.7 0.7 %copy-start.9 = (s32[4,1]{0,1:T(1,128)S(1)}, s32[4,1]{0,1:T(1,128)}, u32[]{:S(2)}) copy-start(s32[4,1]{0,1:T(1,128)} %param.14) | copy-start | bytes 52
  0.7 0.7 %copy-start.10 = (s32[4,1]{0,1:T(1,128)S(1)}, s32[4,1]{0,1:T(1,128)}, u32[]{:S(2)}) copy-start(s32[4,1]{0,1:T(1,128)} %param.15) | copy-start | bytes 52
  0.7 0.7 %copy-start.6 = (s32[2,4]{1,0:T(2,128)S(1)}, s32[2,4]{1,0:T(2,128)}, u32[]{:S(2)}) copy-start(s32[2,4]{1,0:T(2,128)} %tilt_ref.1) | copy-start | bytes 100
  0.7 0.7 %copy-start.8 = (s32[4,1]{0,1:T(1,128)S(1)}, s32[4,1]{0,1:T(1,128)}, u32[]{:S(2)}) copy-start(s32[4,1]{0,1:T(1,128)} %param.13) | copy-start | bytes 52
  1.4 1.2 %copy-start = (f32[4,2,128,256]{3,2,1,0:T(8,128)S(1)}, f32[4,2,128,256]{3,2,1,0:T(8,128)}, u32[]{:S(2)}) copy-start(f32[4,2,128,256]{3,2,1,0:T(8,128)} %scat.1) | copy-start | bytes 3145732
  2.6 0.9 %copy-start.1 = (f32[4,1,128,128]{3,2,1,0:T(8,128)S(1)}, f32[4,1,128,128]{3,2,1,0:T(8,128)}, u32[]{:S(2)}) copy-start(f32[4,1,128,128]{3,2,1,0:T(8,128)} %meas.1) | copy-start | bytes 786436
  3.6 0.9 %copy-start.2 = (bf16[2,256,256]{2,1,0:T(8,128)(2,1)S(1)}, bf16[2,256,256]{2,1,0:T(8,128)(2,1)}, u32[]{:S(2)}) copy-start(bf16[2,256,256]{2,1,0:T(8,128)(2,1)} %constant.8.clone.low_ref) | copy-start | bytes 786436
  4.5 0.9 %copy-start.3 = (bf16[2,256,256]{2,1,0:T(8,128)(2,1)S(1)}, bf16[2,256,256]{2,1,0:T(8,128)(2,1)}, u32[]{:S(2)}) copy-start(bf16[2,256,256]{2,1,0:T(8,128)(2,1)} %constant.7.clone.high_ref) | copy-start | bytes 786436
  5.5 0.9 %copy-start.4 = (f32[128,256]{1,0:T(8,128)S(1)}, f32[128,256]{1,0:T(8,128)}, u32[]{:S(2)}) copy-start(f32[128,256]{1,0:T(8,128)} %pot.1) | copy-start | bytes 393220

commit v8 on v7

--- a/solution.py
+++ b/solution.py
@@ -53,6 +53,19 @@
 def kernel(
     n,
     tiles,
+    row_in,
+    col_in,
+    index_in,
+    tilt_in,
+    coef_in,
+    trig_in,
+    high_in,
+    low_in,
+    scat_in,
+    pot_in,
+    meas,
+    misfit_ref,
+    grad_ref,
     row_ref,
     col_ref,
     index_ref,
@@ -63,9 +76,6 @@
     low_ref,
     scat,
     pot,
-    meas,
-    misfit_ref,
-    grad_ref,
     halo,
     phalo,
     seen,
@@ -92,16 +102,10 @@
 ):
     me = lax.axis_index("beam")
     tile = lax.axis_index("tile")
-    beams = scat.shape[0]
-    rows, cols = scat.shape[2], scat.shape[3]
+    beams = scat_in.shape[0]
+    rows, cols = scat_in.shape[2], scat_in.shape[3]
     patch = seen.shape[-1]
     early = patch - MARGIN
-
-    local = [
-        pltpu.make_async_copy(meas.at[me, 0], seen, local_sem.at[0]),
-    ]
-    for copy in local:
-        copy.start()
 
     barrier = pltpu.get_barrier_semaphore()
     for k in range(1, n):
@@ -118,6 +122,25 @@
     @pl.when(has_down)
     def _():
         pl.semaphore_signal(barrier, inc=1, device_id={"tile": tile + 1}, device_id_type=MESH)
+
+    pairs = [
+        (scat_in, scat),
+        (row_in, row_ref),
+        (col_in, col_ref),
+        (index_in, index_ref),
+        (tilt_in, tilt_ref),
+        (coef_in, coef_ref),
+        (trig_in, trig_ref),
+        (pot_in, pot),
+        (meas.at[me, 0], seen),
+        (high_in, high_ref),
+        (low_in, low_ref),
+    ]
+    local = [
+        pltpu.make_async_copy(src, dst, local_sem.at[i]) for i, (src, dst) in enumerate(pairs)
+    ]
+    for copy in local:
+        copy.start()
 
     def weights(p):
         corner = row_ref[p] + tile * rows - MARGIN
@@ -190,6 +213,8 @@
         block[k, 0] = got[:, :patch]
         block[k, 1] = got[:, patch:]
 
+    for copy in local[:7]:
+        copy.wait()
     make_block(order[0])
 
     pl.semaphore_wait(barrier, n - 1 + has_up.astype(jnp.int32) + has_down.astype(jnp.int32))
@@ -209,12 +234,12 @@
     second = pl.ds(MARGIN, MARGIN)
     below = pl.ds(rows + MARGIN, MARGIN)
     up = [
-        remote(scat.at[:, :, first, :], halo.at[:, :, second, :], halo_send.at[0], halo_recv.at[0], {"tile": tile - 1}),
-        remote(pot.at[first, :], phalo.at[second, :], halo_send.at[1], halo_recv.at[1], {"tile": tile - 1}),
+        remote(scat_in.at[:, :, first, :], halo.at[:, :, second, :], halo_send.at[0], halo_recv.at[0], {"tile": tile - 1}),
+        remote(pot_in.at[first, :], phalo.at[second, :], halo_send.at[1], halo_recv.at[1], {"tile": tile - 1}),
     ]
     down = [
-        remote(scat.at[:, :, last, :], halo.at[:, :, first, :], halo_send.at[2], halo_recv.at[2], {"tile": tile + 1}),
-        remote(pot.at[last, :], phalo.at[first, :], halo_send.at[3], halo_recv.at[3], {"tile": tile + 1}),
+        remote(scat_in.at[:, :, last, :], halo.at[:, :, first, :], halo_send.at[2], halo_recv.at[2], {"tile": tile + 1}),
+        remote(pot_in.at[last, :], phalo.at[first, :], halo_send.at[3], halo_recv.at[3], {"tile": tile + 1}),
     ]
 
     @pl.when(has_up)
@@ -275,6 +300,7 @@
             )
             copies_b[k].start()
 
+    local[7].wait()
     tall = jnp.concatenate([pot[...], phalo[...]], 0)
     high, low = split(tall)
     least = (tall - high.astype(jnp.float32) - low.astype(jnp.float32)).astype(jnp.bfloat16)
@@ -290,7 +316,8 @@
     for k in order:
         copies_a[k].wait_recv()
         copies_b[k].wait_recv()
-    local[0].wait()
+    for copy in local[8:]:
+        copy.wait()
 
     parts = []
     for c in range(2):
@@ -400,9 +427,10 @@
     positions, patch = measured.shape[0], measured.shape[-1]
     assert positions == n and patch & (patch - 1) == 0 and cols & (cols - 1) == 0
     high, low, trig = tables(patch)
+    coefs = coef_table.reshape(-1, beams)
     f32 = jnp.float32
     early = patch - MARGIN
-    smem = pl.BlockSpec(memory_space=pltpu.SMEM)
+    i32 = jnp.int32
     vmem = pl.BlockSpec(memory_space=pltpu.VMEM)
     anywhere = pl.BlockSpec(memory_space=pl.ANY)
     strip_rows = rows + 2 * MARGIN
@@ -413,9 +441,19 @@
             jax.ShapeDtypeStruct((patch, patch), f32),
             jax.ShapeDtypeStruct((rows, cols), f32),
         ),
-        in_specs=[smem] * 6 + [vmem] * 4 + [anywhere],
+        in_specs=[anywhere] * 11,
         out_specs=(vmem, vmem),
         scratch_shapes=[
+            pltpu.SMEM((n,), i32),
+            pltpu.SMEM((n,), i32),
+            pltpu.SMEM((n,), i32),
+            pltpu.SMEM((2, beams), i32),
+            pltpu.SMEM(coefs.shape, f32),
+            pltpu.SMEM(trig.shape, f32),
+            pltpu.VMEM(high.shape, jnp.bfloat16),
+            pltpu.VMEM(low.shape, jnp.bfloat16),
+            pltpu.VMEM((beams, 2, rows, cols), f32),
+            pltpu.VMEM((rows, cols), f32),
             pltpu.VMEM((beams, 2, 2 * MARGIN, cols), f32),
             pltpu.VMEM((2 * MARGIN, cols), f32),
             pltpu.VMEM((patch, patch), f32),
@@ -428,7 +466,7 @@
             pltpu.VMEM((n - 1, patch, patch), f32),
             pltpu.VMEM((strip_rows, cols), f32),
             pltpu.VMEM((2, MARGIN, cols), f32),
-            dma((1,)),
+            dma((11,)),
             dma((4,)),
             dma((4,)),
             dma((n - 1,)),
@@ -441,14 +479,14 @@
             dma((2,)),
         ],
         compiler_params=pltpu.CompilerParams(
-            collective_id=0, has_side_effects=True, vmem_limit_bytes=12 * 1024 * 1024
+            collective_id=0, has_side_effects=True, vmem_limit_bytes=56 * 1024 * 1024
         ),
     )(
         row_offset[:, 0],
         col_offset[:, 0],
         table_index[:, 0],
         beam_tilt,
-        coef_table.reshape(-1, beams),
+        coefs,
         trig,
         high,
         low,

time: 37 us -> 32.1 us (0.87)
  local copies, waits for them, and re-layouts: 6.96 us -> 2.17 us
    unnamed x24 -> x4, local copies, waits for them, and re-layouts: 6.96 us -> 2.17 us
where the time goes in v8:
time: 32.1 us; the launch traced here: 31.9 us
  Pallas kernels  29.1 us (91%)
  local copies, waits for them, and re-layouts  2.17 us (7%)
  between operations  0.65 us (2%)
    pallas_call x1, Pallas kernels, shards(): pl.pallas_call(functools.partial(kernel, n, tiles), out_shape=(jax.ShapeD...  29.1 us
    unnamed x4, local copies, waits for them, and re-layouts  2.17 us

profile of v8, /device:TPU:1, one launch (start us, length us, event | category | flops | bytes accessed | tf_op | source)
XLA Modules:
  0.0 31.9 jit_solution(10446703969702030489)
XLA Ops:
  0.6 29.1 %shard_map.122 = (f32[128,128]{1,0:T(8,128)}, f32[128,256]{1,0:T(8,128)}) custom-call(s32[4]{0:T(128)} %bitcast.7, s32[4]{0:T(128)} %bitcast.8, s32[4]{0:T(128)} %bitcast.9, s32[2,4]{1,0:T(2,128)} %tilt_in.1, f32[8,4]{1,0:T(8,128)} %bitcast.6, f32[2,128]{1,0:T(2,128)} %constant.6.clone.trig_in, bf16[2,256,256]{2,1,0:T(8,128)(2,1)} %constant.7.clone.high_in, ...), custom_call_target="tpu_custom_call" | custom-call | tf_op jit(solution)/shard_map/pallas_call | solution.py:438
  29.8 0.0 copy-start
  29.8 1.5 %copy.18 = f32[1,1,128,128]{3,2,1,0:T(8,128)} copy(f32[1,1,128,128]{3,2,1,0:T(8,128)} %bitcast.5) | data formatting | bytes 131072
  31.3 0.0 copy-done
  31.3 0.7 %copy.19 = f32[128,256]{1,0:T(8,128)} copy(f32[128,256]{1,0:T(8,128)S(1)} %copy-done) | data formatting | bytes 262144
Async XLA Ops:
  29.8 1.5 %copy-start = (f32[128,256]{1,0:T(8,128)S(1)}, f32[128,256]{1,0:T(8,128)}, u32[]{:S(2)}) copy-start(f32[128,256]{1,0:T(8,128)} %get-tuple-element.9) | copy-start | bytes 393220

commit v9 on v8

--- a/solution.py
+++ b/solution.py
@@ -409,6 +409,19 @@
     def _():
         for copy in down + [rim_down]:
             copy.wait_send()
+
+
+def hand_over(misfit_in, grad_in, misfit_out, grad_out, misfit, grad, sem):
+    pairs = [(misfit_in, misfit, misfit_out), (grad_in, grad, grad_out)]
+    ins = [pltpu.make_async_copy(a, b, sem.at[0, i]) for i, (a, b, _) in enumerate(pairs)]
+    outs = [pltpu.make_async_copy(b, c, sem.at[1, i]) for i, (_, b, c) in enumerate(pairs)]
+    for copy in ins:
+        copy.start()
+    for here, there in zip(ins, outs):
+        here.wait()
+        there.start()
+    for copy in outs:
+        copy.wait()
 
 
 def shards(
@@ -494,6 +507,15 @@
         potential,
         measured,
     )
+    shapes = (jax.ShapeDtypeStruct((patch, patch), f32), jax.ShapeDtypeStruct((rows, cols), f32))
+    misfit, grad = pl.pallas_call(
+        hand_over,
+        out_shape=shapes,
+        in_specs=[anywhere] * 2,
+        out_specs=(anywhere, anywhere),
+        scratch_shapes=[pltpu.VMEM(shape.shape, f32) for shape in shapes] + [dma((2, 2))],
+        compiler_params=pltpu.CompilerParams(vmem_limit_bytes=56 * 1024 * 1024),
+    )(misfit, grad)
     return misfit[None, None], grad
 
 

time: 32.1 us -> 31.6 us (0.984)
  local copies, waits for them, and re-layouts: 2.17 us -> 0 us
  Pallas kernels: 29.1 us -> 30.8 us
    unnamed x4 -> x0, local copies, waits for them, and re-layouts: 2.17 us -> none
    pallas_call x0 -> x1, Pallas kernels: none -> 1.63 us  [shards(): pl.pallas_call(hand_over, out_shape=shapes, in_specs=[anywhere] * 2, out_...]
where the time goes in v9:
time: 31.6 us; the launch traced here: 31.4 us
  Pallas kernels  30.8 us (97%)
  between operations  0.64 us (2%)
    pallas_call x1, Pallas kernels, shards(): pl.pallas_call(functools.partial(kernel, n, tiles), out_shape=(jax.ShapeD...  29.1 us
    pallas_call x1, Pallas kernels, shards(): pl.pallas_call(hand_over, out_shape=shapes, in_specs=[anywhere] * 2, out_...  1.63 us

profile of v9, /device:TPU:1, one launch (start us, length us, event | category | flops | bytes accessed | tf_op | source)
XLA Modules:
  0.0 31.4 jit_solution(14846693641387959059)
XLA Ops:
  0.6 29.1 %shard_map.122 = (f32[128,128]{1,0:T(8,128)}, f32[128,256]{1,0:T(8,128)}) custom-call(s32[4]{0:T(128)} %bitcast.6, s32[4]{0:T(128)} %bitcast.7, s32[4]{0:T(128)} %bitcast.8, s32[2,4]{1,0:T(2,128)} %tilt_in.1, f32[8,4]{1,0:T(8,128)} %bitcast.5, f32[2,128]{1,0:T(2,128)} %constant.6.clone.trig_in, bf16[2,256,256]{2,1,0:T(8,128)(2,1)} %constant.7.clone.high_in, ...), custom_call_target="tpu_custom_call" | custom-call | tf_op jit(solution)/shard_map/pallas_call | solution.py:451
  29.8 1.6 %shard_map.123 = (f32[128,128]{1,0:T(8,128)}, f32[128,256]{1,0:T(8,128)}) custom-call(f32[128,128]{1,0:T(8,128)} %get-tuple-element.6.misfit_in, f32[128,256]{1,0:T(8,128)} %get-tuple-element.7.grad_in), custom_call_target="tpu_custom_call" | custom-call | tf_op jit(solution)/shard_map/pallas_call | solution.py:511
